TPU v7x, 512 devices: a whole 4x8x8 slice. The times are simulated.
512 devices in a mesh: layer: 16 (over x, y_hi, core), dp: 32 (over y_lo, z).
Axes of the slice: x: 4, y: 8 (y_hi: 2, y_lo: 4; y = y_hi * 4 + y_lo), z: 8, core: 2. Of those that a mesh axis runs over, the one named last changes fastest.
Arguments:
- acts: bfloat16 [16, 8192, 4096], P('layer', 'dp'), may hold values from -6 to 6
- factor_old: bfloat16 [16, 4096, 4096], P('layer', 'dp'), as said below
- basis_old: bfloat16 [16, 4096, 256], P('layer', 'dp'), may hold values from -0.09375 to 0.09375
- grads: bfloat16 [16, 4096, 2048], P(None, 'dp', 'layer'), may hold values from -12 to 12
Outputs:
- new_basis: bfloat16 [16, 4096, 256], P('layer', 'dp')
- eigenvalues: bfloat16 [16, 256], P('layer')
- preconditioned: bfloat16 [16, 4096, 2048], P(None, 'dp', 'layer')
- applied_rows: float32 [16, 4096, 256], P('layer', 'dp')
Inputs may be any that keep to these rules, and one draw needn't show every extreme that they name: `factor_old`: each block is symmetric with a positive diagonal that outweighs the spectral norm of its off-diagonal part.
All inputs are finite; a program needn't handle non-finite values.
Results may differ from a plain program's by a relative error of at most 0.0035.
Values may be sent and summed in bfloat16 or wider, within the bound.
No kernel may reach another device: no remote copies, remote signals or barrier semaphores. Data moves between devices by JAX's collectives and lax.ppermute only.
A program may use at most 64 MiB of HBM per device.

v0:
```python
import math

import jax
import jax.numpy as jnp
from jax import lax
from jax.sharding import PartitionSpec as P

decay_rate = 0.25
damping = 2.0


def per_device(acts, factor_old, basis_old, grads):
    old_basis = lax.all_gather(basis_old, "dp", axis=1, tiled=True)[0]
    token_rows = acts[0]
    projected = jnp.dot(token_rows, old_basis, preferred_element_type=jnp.float32).astype(
        jnp.bfloat16
    )
    summed = lax.psum_scatter(
        lax.dot_general(
            token_rows, projected, (((0,), (0,)), ((), ())), preferred_element_type=jnp.float32
        ),
        "dp",
        scatter_dimension=0,
        tiled=True,
    )
    total_tokens = token_rows.shape[0] * lax.axis_size("dp")
    applied = (
        decay_rate * jnp.dot(factor_old[0], old_basis, preferred_element_type=jnp.float32)
        + (1.0 - decay_rate) / total_tokens * summed
    )
    applied_rows = applied * math.sqrt(factor_old.shape[2])
    gram_local = jnp.dot(applied.T, applied, precision=lax.Precision.HIGHEST)
    gram_total = lax.psum(gram_local, "dp")
    lower = jnp.linalg.cholesky(gram_total)
    eigen_vals = jnp.diagonal(lower).astype(jnp.bfloat16)
    solved = lax.linalg.triangular_solve(
        lower, applied, left_side=False, lower=True, transpose_a=True
    )
    fresh = solved.astype(jnp.bfloat16)
    slab = lax.all_to_all(grads, "layer", split_axis=0, concat_axis=2, tiled=True)[0]
    coupling_local = lax.dot_general(
        fresh, slab, (((0,), (0,)), ((), ())), preferred_element_type=jnp.float32
    )
    coupling = lax.psum(coupling_local, "dp")
    factors = 1.0 / (eigen_vals.astype(jnp.float32) + damping) - 1.0 / damping
    scaled = (factors[:, None] * coupling).astype(jnp.bfloat16)
    result = slab.astype(jnp.float32) / damping + jnp.dot(
        fresh, scaled, preferred_element_type=jnp.float32
    )
    conditioned = lax.all_to_all(
        result.astype(jnp.bfloat16)[None], "layer", split_axis=2, concat_axis=0, tiled=True
    )
    return (fresh[None], eigen_vals[None], conditioned, applied_rows[None])


def solution(mesh):
    in_specs = (
        P("layer", "dp", None),
        P("layer", "dp", None),
        P("layer", "dp", None),
        P(None, "dp", "layer"),
    )
    out_specs = (
        P("layer", "dp", None),
        P("layer", None),
        P(None, "dp", "layer"),
        P("layer", "dp", None),
    )
    return jax.shard_map(
        per_device, mesh=mesh, in_specs=in_specs, out_specs=out_specs, check_vma=False
    )
```

profile of v0, /device:TPU:1, one launch (start us, length us, event | category | flops | bytes accessed | tf_op | source)
XLA Modules:
  0.0 1075.7 jit_solution(997168262411807323)
XLA Ops:
  7.2 0.0 all-gather.2.cloned.1.call-start
  7.2 0.7 all-gather.2.cloned.1.call-update
  7.9 0.0 reduce-scatter.2.cloned.1.call-start
  8.0 142.2 %all-gather.2.cloned.1.call-done = bf16[1,4096,256]{2,1,0:T(8,128)(2,1)} async-done(((bf16[1,128,256]{2,1,0:T(8,128)(2,1)}), bf16[1,4096,256]{2,1,0:T(8,128)(2,1)}) %all-gather.2.cloned.1.call-update) | async-done | bytes 2097168 | tf_op jit(solution)/shard_map/all_gather | solution.py:13
  150.2 6.0 convolution_bitcast_fusion
  156.1 28.7 %all-to-all-start = ((bf16[16,128,128]{2,1,0:T(8,128)(2,1)}), bf16[16,128,128]{2,1,0:T(8,128)(2,1)}, u32[]{:S(2)}, u32[]{:S(2)}) async-start(bf16[16,128,128]{2,1,0:T(8,128)(2,1)} %param.7), calls=%async_computation.1 | async-start | bytes 1048576 | tf_op jit(solution)/shard_map/all_to_all | solution.py:40
  184.9 0.0 all-reduce.4.cloned.1.call-start
  184.9 136.2 %reduce-scatter.2.cloned.1.call-done = f32[128,256]{1,0:T(8,128)} async-done(((f32[4096,256]{1,0:T(8,128)}), f32[128,256]{1,0:T(8,128)}) %reduce-scatter.2.cloned.1.call-update) | async-done | bytes 131088 | tf_op jit(solution)/shard_map/reduce_scatter | solution.py:18
  321.1 2.0 fusion.20
  323.1 1.1 fusion.40
  324.3 0.2 all-reduce.6.cloned.1.call-start
  324.5 1.4 copy.30
  325.9 297.8 %all-reduce.4.cloned.1.call-done = f32[256,256]{0,1:T(8,128)} async-done(((f32[256,256]{0,1:T(8,128)}), f32[256,256]{0,1:T(8,128)}) %all-reduce.4.cloned.1.call-update) | async-done | bytes 262160 | tf_op jit(solution)/shard_map/psum | solution.py:33
  623.7 1.1 copy.29
  624.8 1.0 fusion.28
  625.8 0.7 copy-done.2
  626.5 11.7 %cholesky.50 = f32[128,128]{1,0:T(8,128)S(1)} custom-call(f32[128,128]{1,0:T(8,128)S(1)} %cholesky.118), custom_call_target="Cholesky" | custom-call | tf_op jit(solution)/shard_map/jit(cholesky)/cholesky | solution.py:34
  638.2 9.8 custom-call.14
  648.1 1.0 constant_dynamic-update-slice_fusion.1
  649.1 1.1 convolution_subtract_fusion.1
  650.2 11.7 %cholesky.105 = f32[128,128]{1,0:T(8,128)S(1)} custom-call(f32[128,128]{1,0:T(8,128)S(1)} %convolution_subtract_fusion.1), custom_call_target="Cholesky" | custom-call | tf_op jit(solution)/shard_map/jit(cholesky)/cholesky | solution.py:34
  662.0 0.6 compare_reduce_fusion
  664.0 0.1 triangular_solve.64
  664.0 5.4 while.1
  664.2 0.6 fusion.48
  664.8 2.0 bitcast_dynamic-update-slice_fusion.2
  666.8 0.6 fusion.48
  667.4 2.0 bitcast_dynamic-update-slice_fusion.2
  669.4 20.5 %custom-call.15 = f32[2,128,128]{1,2,0:T(8,128)S(1)} custom-call(f32[2,128,128]{2,1,0:T(8,128)} %get-tuple-element.11), custom_call_target="InvertDiagBlocksLowerTriangular" | custom-call | tf_op jit(solution)/shard_map/triangular_solve | solution.py:36
  689.9 0.3 fusion.39
  690.2 0.3 convolution_subtract_fusion
  690.5 0.3 convolution_convert_fusion
  690.8 1.7 fusion.25
  692.6 2.5 gather_fusion
  695.1 305.5 %all-reduce.6.cloned.1.call-done = f32[256,2048]{1,0:T(8,128)} async-done(((f32[256,2048]{1,0:T(8,128)}), f32[256,2048]{1,0:T(8,128)}) %all-reduce.6.cloned.1.call-update) | async-done | bytes 2097168 | tf_op jit(solution)/shard_map/psum | solution.py:44
  1000.6 2.8 fusion.1
  1003.4 2.3 copy.31
  1005.8 0.5 broadcast.146
  1006.3 12.3 %reduce.12 = bf16[2048,128]{1,0:T(8,128)(2,1)} reduce(bf16[2048,1,128]{2,1,0:T(2,128)(2,1)S(1)} %bitcast.89, bf16[]{:T(256)} %broadcast.146), dimensions={1}, to_apply=%bitcast.67.reduce_sub_computation | reduce | bytes 1048578
  1018.6 1.9 reshape.97
  1020.6 29.7 %all-to-all-start.1 = ((bf16[16,2,8192]{2,1,0:T(2,128)(2,1)}), bf16[16,2,8192]{2,1,0:T(2,128)(2,1)}, u32[]{:S(2)}, u32[]{:S(2)}) async-start(bf16[16,2,8192]{2,1,0:T(2,128)(2,1)} %reshape.97), calls=%async_computation.2 | async-start | bytes 1048576 | tf_op jit(solution)/shard_map/all_to_all | solution.py:50
  1050.3 0.7 multiply_bitcast_fusion
  1050.9 0.6 convert_element_type.46
  1051.5 0.7 copy.32
  1052.3 11.8 %all-to-all-done.1 = bf16[16,2,8192]{2,1,0:T(2,128)(2,1)} async-done(((bf16[16,2,8192]{2,1,0:T(2,128)(2,1)}), bf16[16,2,8192]{2,1,0:T(2,128)(2,1)}, u32[]{:S(2)}, u32[]{:S(2)}) %all-to-all-start.1) | async-done | bytes 524320 | tf_op jit(solution)/shard_map/all_to_all | solution.py:50
  1064.1 2.2 reshape.98
  1066.3 0.9 copy.36
  1067.2 2.0 copy.33
  (21 shorter events, 0.2 us)
Async XLA Ops:
  7.2 143.0 %copy-start = (bf16[1,256,4096]{2,1,0:T(8,128)(2,1)S(1)}, bf16[1,256,4096]{2,1,0:T(8,128)(2,1)}, u32[]{:S(2)}) copy-start(bf16[1,256,4096]{2,1,0:T(8,128)(2,1)} %param.4) | copy-start | bytes 6291460
  7.2 143.0 %all-gather.2.cloned.1.call-start = ((), (), s32[]{:S(2)}) async-start(), calls=%async_computation.3 | async-start | bytes 2162688 | tf_op jit(solution)/shard_map/all_gather | solution.py:13
  7.9 313.2 %reduce-scatter.2.cloned.1.call-start = ((), (), s32[]{:S(2)}) async-start(), calls=%async_computation.4 | async-start | bytes 4325376 | tf_op jit(solution)/shard_map/reduce_scatter | solution.py:18
  156.1 165.0 %copy-start.1 = (bf16[1,128,4096]{2,1,0:T(8,128)(2,1)S(1)}, bf16[1,128,4096]{2,1,0:T(8,128)(2,1)}, u32[]{:S(2)}) copy-start(bf16[1,128,4096]{2,1,0:T(8,128)(2,1)} %param.5) | copy-start | bytes 3145732
  156.1 168.4 %all-to-all-start = ((bf16[16,128,128]{2,1,0:T(8,128)(2,1)}), bf16[16,128,128]{2,1,0:T(8,128)(2,1)}, u32[]{:S(2)}, u32[]{:S(2)}) async-start(bf16[16,128,128]{2,1,0:T(8,128)(2,1)} %param.7), calls=%async_computation.1 | async-start | bytes 1048576 | tf_op jit(solution)/shard_map/all_to_all | solution.py:40
  184.9 438.8 %all-reduce.4.cloned.1.call-start = ((), (), s32[]{:S(2)}) async-start(), calls=%async_computation.5 | async-start | bytes 524288 | tf_op jit(solution)/shard_map/psum | solution.py:33
  324.3 676.4 %all-reduce.6.cloned.1.call-start = ((), (), s32[]{:S(2)}) async-start(), calls=%async_computation.6 | async-start | bytes 4194304 | tf_op jit(solution)/shard_map/psum | solution.py:44
  625.8 0.7 copy-start.2
  1020.6 43.5 %all-to-all-start.1 = ((bf16[16,2,8192]{2,1,0:T(2,128)(2,1)}), bf16[16,2,8192]{2,1,0:T(2,128)(2,1)}, u32[]{:S(2)}, u32[]{:S(2)}) async-start(bf16[16,2,8192]{2,1,0:T(2,128)(2,1)} %reshape.97), calls=%async_computation.2 | async-start | bytes 1048576 | tf_op jit(solution)/shard_map/all_to_all | solution.py:50
Sparse Core Ops, SparseCore 0:
  10.1 140.0 all-gather.1
  156.3 164.7 reduce-scatter.1
  324.6 299.0 all-reduce.3
  692.7 307.8 all-reduce.5
where the time goes:
time: 1080 us
  waiting for transfers between devices  894 us (83%)
  other arithmetic  68.5 us (6%)
  starting transfers between devices  58.8 us (5%)
  local copies, waits for them, and re-layouts  22.2 us (2%)
  matrix products  16.6 us (2%)
  between operations  15.2 us (1%)
    psum x1, waiting for transfers between devices, per_device(): coupling = lax.psum(coupling_local, 'dp')  306 us
    psum x1, waiting for transfers between devices, per_device(): gram_total = lax.psum(gram_local, 'dp')  298 us
    all_gather x1, waiting for transfers between devices, per_device(): old_basis = lax.all_gather(basis_old, 'dp', axis=1, tiled=True)[0]  142 us
    reduce_scatter x1, waiting for transfers between devices, per_device(): lax.psum_scatter(lax.dot_general(token_rows, projected, (((0,), (0,)), ((...  136 us
    another operation x6, other arithmetic, per_device(): lower = jnp.linalg.cholesky(gram_total)  34 us
    all_to_all x1, starting transfers between devices, per_device(): lax.all_to_all(result.astype(jnp.bfloat16)[None], 'layer', split_axis=2,...  29.7 us
    all_to_all x1, starting transfers between devices, per_device(): lax.all_to_all(grads, 'layer', split_axis=0, concat_axis=2, tiled=True)[0]  28.7 us
  transfers between devices with their start and end apart: 6, of which 5 were waited for; matrix products, arithmetic and copies ran while one was open for 1% of the time, Pallas kernels for 0%

commit v1 on v0

v1 whole, which is shorter than its diff:
```python
import math

import jax
import jax.numpy as jnp
from jax import lax
from jax.sharding import PartitionSpec as P

decay_rate = 0.25
damping = 2.0
HIGHEST = lax.Precision.HIGHEST


def exchange(parts, axis):
    return lax.all_to_all(parts, axis, split_axis=0, concat_axis=0, tiled=True)


def gather(part, axis, copies):
    return exchange(jnp.broadcast_to(part[None], (copies,) + part.shape), axis)


def per_device(acts, factor_old, basis_old, grads):
    ranks = lax.axis_size("dp")
    token_rows, factor_rows = acts[0], factor_old[0]
    rank = basis_old.shape[2]
    width = factor_rows.shape[1]
    old_basis = gather(basis_old[0], "dp", ranks).reshape(width, rank)
    slab = exchange(grads, "layer")
    projected = jnp.dot(token_rows, old_basis, preferred_element_type=jnp.float32).astype(
        jnp.bfloat16
    )
    partial_sums = lax.dot_general(
        token_rows, projected, (((0,), (0,)), ((), ())), preferred_element_type=jnp.float32
    ).astype(jnp.bfloat16)
    parts = exchange(partial_sums.reshape(ranks, width // ranks, rank), "dp")
    summed = jnp.sum(parts.astype(jnp.float32), axis=0)
    total_tokens = token_rows.shape[0] * ranks
    applied = (
        decay_rate * jnp.dot(factor_rows, old_basis, preferred_element_type=jnp.float32)
        + (1.0 - decay_rate) / total_tokens * summed
    )
    applied_rows = applied * math.sqrt(width)
    gram_local = jnp.dot(applied.T, applied, precision=HIGHEST)
    gram_parts = exchange(gram_local.reshape(ranks, rank // ranks, rank), "dp")
    gram_rows = jnp.sum(gram_parts, axis=0)
    gram_total = gather(gram_rows, "dp", ranks).reshape(rank, rank)

    high = applied.astype(jnp.bfloat16)
    low = (applied - high.astype(jnp.float32)).astype(jnp.bfloat16)
    dims = (((1,), (0,)), ((), ()))
    cross = lax.dot_general(slab, high, dims, preferred_element_type=jnp.float32)
    cross = cross + lax.dot_general(slab, low, dims, preferred_element_type=jnp.float32)
    columns = slab.shape[0] * slab.shape[2]
    cross_parts = exchange(cross.reshape(ranks, columns // ranks, rank), "dp")
    cross_sum = jnp.sum(cross_parts, axis=0)

    lower = jnp.linalg.cholesky(gram_total)
    inverse = lax.linalg.triangular_solve(
        lower, jnp.eye(rank, dtype=jnp.float32), left_side=True, lower=True
    )
    eigen_vals = jnp.diagonal(lower).astype(jnp.bfloat16)
    fresh = lax.dot_general(
        applied, inverse, (((1,), (1,)), ((), ())), precision=HIGHEST
    ).astype(jnp.bfloat16)
    coupling = lax.dot_general(cross_sum, inverse, (((1,), (1,)), ((), ())), precision=HIGHEST)
    factors = 1.0 / (eigen_vals.astype(jnp.float32) + damping) - 1.0 / damping
    scaled_part = (coupling * factors[None, :]).astype(jnp.bfloat16)
    scaled = gather(scaled_part, "dp", ranks).reshape(slab.shape[0], slab.shape[2], rank)
    moved = lax.dot_general(
        fresh, scaled, (((1,), (2,)), ((), ())), preferred_element_type=jnp.float32
    )
    result = slab.astype(jnp.float32) / damping + jnp.swapaxes(moved, 0, 1)
    conditioned = exchange(result.astype(jnp.bfloat16), "layer")
    return (fresh[None], eigen_vals[None], conditioned, applied_rows[None])


def solution(mesh):
    in_specs = (
        P("layer", "dp", None),
        P("layer", "dp", None),
        P("layer", "dp", None),
        P(None, "dp", "layer"),
    )
    out_specs = (
        P("layer", "dp", None),
        P("layer", None),
        P(None, "dp", "layer"),
        P("layer", "dp", None),
    )
    return jax.shard_map(
        per_device, mesh=mesh, in_specs=in_specs, out_specs=out_specs, check_vma=False
    )
```

time: 1080 us -> 338 us (0.31)
  the two profiles are of different devices: /device:TPU:1 before, /device:TPU:73 now
where the time goes in v1:
time: 338 us; the launch traced here: 337 us
  blocking collectives  118 us (35%)
  waiting for transfers between devices  79.5 us (24%)
  other arithmetic  58.9 us (17%)
  starting transfers between devices  44.7 us (13%)
  local copies, waits for them, and re-layouts  18.4 us (5%)
  matrix products  15.5 us (5%)
    all_to_all x2, blocking collectives, exchange(): return lax.all_to_all(parts, axis, split_axis=0, concat_axis=0, tiled=True)  118 us
    all_to_all x6, waiting for transfers between devices, exchange(): return lax.all_to_all(parts, axis, split_axis=0, concat_axis=0, tiled=True)  79.5 us
    all_to_all x6, starting transfers between devices, exchange(): return lax.all_to_all(parts, axis, split_axis=0, concat_axis=0, tiled=True)  44.7 us
    another operation x6, other arithmetic, per_device(): lower = jnp.linalg.cholesky(gram_total)  33.9 us
    another operation x3, other arithmetic, per_device(): lax.linalg.triangular_solve(lower, jnp.eye(rank, dtype=jnp.float32), left...  20.5 us
  transfers between devices with their start and end apart: 6, of which 5 were waited for; matrix products, arithmetic and copies ran while one was open for 21% of the time, Pallas kernels for 0%

profile of v1, /device:TPU:73, one launch (start us, length us, event | category | flops | bytes accessed | tf_op | source)
XLA Modules:
  0.0 336.8 jit_solution(7825583753976379922)
XLA Ops:
  0.6 1.2 broadcast_in_dim.19
  1.9 61.9 %all_to_all.40 = bf16[32,128,256]{2,1,0:T(8,128)(2,1)} all-to-all(bf16[32,128,256]{2,1,0:T(8,128)(2,1)S(1)} %broadcast_in_dim.19), channel_id=1, replica_groups=mesh['layer'=16,'dp'=32] {'dp'}, dimensions={0} | all-to-all | bytes 4194304 | tf_op jit(solution)/shard_map/all_to_all | solution.py:14
  63.8 5.4 %fusion.3 = bf16[32,32,8,128]{3,2,1,0:T(8,128)(2,1)} fusion(bf16[1,256,4096]{2,1,0:T(8,128)(2,1)S(1)} %copy-done, bf16[4096,256]{1,0:T(8,128)(2,1)} %bitcast.90), kind=kOutput, calls=%fused_computation.9 | convolution fusion | flops 1074855936 | bytes 6291456 | tf_op jit(solution)/shard_map/dot_general | solution.py:31
  69.2 2.2 copy.27
  71.3 55.7 %all_to_all.41 = bf16[32,128,256]{1,2,0:T(8,128)(2,1)S(1)} all-to-all(bf16[32,128,256]{1,2,0:T(8,128)(2,1)S(1)} %bitcast.96), channel_id=1, replica_groups=mesh['layer'=16,'dp'=32] {'dp'}, dimensions={0} | all-to-all | bytes 4194304 | tf_op jit(solution)/shard_map/all_to_all | solution.py:14
  127.0 0.3 convert_reduce_fusion
  127.4 0.8 copy-done.1
  128.3 2.0 fusion.11
  130.3 1.1 convolution_bitcast_fusion.1
  131.4 6.4 %all-to-all-start.2 = ((f32[32,8,256]{2,1,0:T(8,128)}), f32[32,8,256]{2,1,0:T(8,128)S(1)}, u32[]{:S(2)}, u32[]{:S(2)}) async-start(f32[32,8,256]{2,1,0:T(8,128)} %convolution_bitcast_fusion.1), calls=%async_computation.2 | async-start | bytes 524288 | tf_op jit(solution)/shard_map/all_to_all | solution.py:14
  137.8 2.0 copy.20
  139.8 7.4 %all-to-all-done.2 = f32[32,8,256]{2,1,0:T(8,128)S(1)} async-done(((f32[32,8,256]{2,1,0:T(8,128)}), f32[32,8,256]{2,1,0:T(8,128)S(1)}, u32[]{:S(2)}, u32[]{:S(2)}) %all-to-all-start.2) | async-done | bytes 262176 | tf_op jit(solution)/shard_map/all_to_all | solution.py:14
  147.2 11.7 %all-to-all-start.4 = ((bf16[16,128,128]{1,2,0:T(8,128)(2,1)}), bf16[16,128,128]{1,2,0:T(8,128)(2,1)S(1)}, u32[]{:S(2)}, u32[]{:S(2)}) async-start(bf16[16,128,128]{1,2,0:T(8,128)(2,1)} %copy.20), calls=%async_computation.4 | async-start | bytes 1048576 | tf_op jit(solution)/shard_map/all_to_all | solution.py:14
  158.9 19.3 %all-to-all-done.4 = bf16[16,128,128]{1,2,0:T(8,128)(2,1)S(1)} async-done(((bf16[16,128,128]{1,2,0:T(8,128)(2,1)}), bf16[16,128,128]{1,2,0:T(8,128)(2,1)S(1)}, u32[]{:S(2)}, u32[]{:S(2)}) %all-to-all-start.4) | async-done | bytes 524320 | tf_op jit(solution)/shard_map/all_to_all | solution.py:14
  178.2 0.7 broadcast_in_dim.20
  178.9 4.0 %all-to-all-start.3 = ((f32[32,8,256]{2,1,0:T(8,128)}), f32[32,8,256]{2,1,0:T(8,128)S(1)}, u32[]{:S(2)}, u32[]{:S(2)}) async-start(f32[32,8,256]{2,1,0:T(8,128)} %broadcast_in_dim.20), calls=%async_computation.3 | async-start | bytes 524288 | tf_op jit(solution)/shard_map/all_to_all | solution.py:14
  182.9 0.4 fusion.28
  183.3 0.4 fusion.20
  183.7 1.6 add.55
  185.3 6.8 %all-to-all-done.3 = f32[32,8,256]{2,1,0:T(8,128)S(1)} async-done(((f32[32,8,256]{2,1,0:T(8,128)}), f32[32,8,256]{2,1,0:T(8,128)S(1)}, u32[]{:S(2)}, u32[]{:S(2)}) %all-to-all-start.3) | async-done | bytes 262176 | tf_op jit(solution)/shard_map/all_to_all | solution.py:14
  192.1 7.4 %all-to-all-start.5 = ((f32[32,64,256]{2,1,0:T(8,128)}), f32[32,64,256]{2,1,0:T(8,128)}, u32[]{:S(2)}, u32[]{:S(2)}) async-start(f32[32,64,256]{2,1,0:T(8,128)} %bitcast.93), calls=%async_computation.5 | async-start | bytes 4194304 | tf_op jit(solution)/shard_map/all_to_all | solution.py:14
  199.7 0.7 copy-done.2
  200.4 11.7 %cholesky.50 = f32[128,128]{1,0:T(8,128)S(1)} custom-call(f32[128,128]{1,0:T(8,128)S(1)} %cholesky.118), custom_call_target="Cholesky" | custom-call | tf_op jit(solution)/shard_map/jit(cholesky)/cholesky | solution.py:56
  212.2 9.8 %custom-call.14 = f32[1,128,128]{1,2,0:T(8,128)S(1)} custom-call(f32[1,128,128]{2,1,0:T(8,128)S(1)} %get-tuple-element.39), custom_call_target="InvertDiagBlocksLowerTriangular" | custom-call | tf_op jit(solution)/shard_map/jit(cholesky)/cholesky | solution.py:56
  222.0 1.0 constant_dynamic-update-slice_fusion.1
  223.1 1.1 convolution_subtract_fusion.1
  224.2 11.7 %cholesky.105 = f32[128,128]{1,0:T(8,128)S(1)} custom-call(f32[128,128]{1,0:T(8,128)S(1)} %convolution_subtract_fusion.1), custom_call_target="Cholesky" | custom-call | tf_op jit(solution)/shard_map/jit(cholesky)/cholesky | solution.py:56
  235.9 0.6 compare_reduce_fusion
  238.0 5.2 %while.1 = (s32[]{:T(128)}, f32[256,256]{1,0:T(8,128)S(1)}, s32[2,2]{1,0:T(2,128)S(1)}, f32[2,128,128]{2,1,0:T(8,128)}, s32[]{:T(128)}) while((s32[]{:T(128)}, f32[256,256]{1,0:T(8,128)S(1)}, s32[2,2]{1,0:T(2,128)S(1)}, f32[2,128,128]{2,1,0:T(8,128)}, s32[]{:T(128)}) %tuple.32), condition=%wide.while_cond, body=%wide.while_body.sunk | while | flops 2 | bytes 132705 | solution.py:57
  238.0 0.6 fusion.47
  238.6 2.0 bitcast_dynamic-update-slice_fusion.2
  240.6 0.6 fusion.47
  241.2 2.0 bitcast_dynamic-update-slice_fusion.2
  243.2 20.5 %custom-call.15 = f32[2,128,128]{1,2,0:T(8,128)S(1)} custom-call(f32[2,128,128]{2,1,0:T(8,128)} %get-tuple-element.11), custom_call_target="InvertDiagBlocksLowerTriangular" | custom-call | tf_op jit(solution)/shard_map/triangular_solve | solution.py:57
  263.7 2.5 gather_fusion
  266.8 0.3 fusion.22
  267.1 1.7 reduce_sum.29
  268.8 0.4 fusion.12
  269.2 1.1 broadcast_in_dim.37
  270.3 9.6 %all-to-all-start.6 = ((bf16[32,64,256]{2,1,0:T(8,128)(2,1)}), bf16[32,64,256]{2,1,0:T(8,128)(2,1)}, u32[]{:S(2)}, u32[]{:S(2)}) async-start(bf16[32,64,256]{2,1,0:T(8,128)(2,1)} %broadcast_in_dim.37), calls=%async_computation.6 | async-start | bytes 2097152 | tf_op jit(solution)/shard_map/all_to_all | solution.py:14
  280.0 0.4 convolution_convert_fusion.1
  280.4 27.4 %all-to-all-done.6 = bf16[32,64,256]{2,1,0:T(8,128)(2,1)} async-done(((bf16[32,64,256]{2,1,0:T(8,128)(2,1)}), bf16[32,64,256]{2,1,0:T(8,128)(2,1)}, u32[]{:S(2)}, u32[]{:S(2)}) %all-to-all-start.6) | async-done | bytes 1048608 | tf_op jit(solution)/shard_map/all_to_all | solution.py:14
  307.7 2.5 fusion.7
  310.2 5.7 %all-to-all-start.7 = ((bf16[16,128,128]{1,2,0:T(8,128)(2,1)}), bf16[16,128,128]{1,2,0:T(8,128)(2,1)S(1)}, u32[]{:S(2)}, u32[]{:S(2)}) async-start(bf16[16,128,128]{1,2,0:T(8,128)(2,1)} %fusion.7), calls=%async_computation.7 | async-start | bytes 1048576 | tf_op jit(solution)/shard_map/all_to_all | solution.py:14
  315.9 0.7 multiply_bitcast_fusion
  316.5 0.6 convert_element_type.63
  317.1 18.7 %all-to-all-done.7 = bf16[16,128,128]{1,2,0:T(8,128)(2,1)S(1)} async-done(((bf16[16,128,128]{1,2,0:T(8,128)(2,1)}), bf16[16,128,128]{1,2,0:T(8,128)(2,1)S(1)}, u32[]{:S(2)}, u32[]{:S(2)}) %all-to-all-start.7) | async-done | bytes 524320 | tf_op jit(solution)/shard_map/all_to_all | solution.py:14
  335.8 1.0 copy.22
  (26 shorter events, 1.1 us)
Async XLA Ops:
  0.6 63.2 %copy-start = (bf16[1,256,4096]{2,1,0:T(8,128)(2,1)S(1)}, bf16[1,256,4096]{2,1,0:T(8,128)(2,1)}, u32[]{:S(2)}) copy-start(bf16[1,256,4096]{2,1,0:T(8,128)(2,1)} %param.4) | copy-start | bytes 6291460
  127.0 1.2 copy-start.1
  131.4 15.8 %all-to-all-start.2 = ((f32[32,8,256]{2,1,0:T(8,128)}), f32[32,8,256]{2,1,0:T(8,128)S(1)}, u32[]{:S(2)}, u32[]{:S(2)}) async-start(f32[32,8,256]{2,1,0:T(8,128)} %convolution_bitcast_fusion.1), calls=%async_computation.2 | async-start | bytes 524288 | tf_op jit(solution)/shard_map/all_to_all | solution.py:14
  147.2 31.0 %all-to-all-start.4 = ((bf16[16,128,128]{1,2,0:T(8,128)(2,1)}), bf16[16,128,128]{1,2,0:T(8,128)(2,1)S(1)}, u32[]{:S(2)}, u32[]{:S(2)}) async-start(bf16[16,128,128]{1,2,0:T(8,128)(2,1)} %copy.20), calls=%async_computation.4 | async-start | bytes 1048576 | tf_op jit(solution)/shard_map/all_to_all | solution.py:14
  178.9 13.2 %all-to-all-start.3 = ((f32[32,8,256]{2,1,0:T(8,128)}), f32[32,8,256]{2,1,0:T(8,128)S(1)}, u32[]{:S(2)}, u32[]{:S(2)}) async-start(f32[32,8,256]{2,1,0:T(8,128)} %broadcast_in_dim.20), calls=%async_computation.3 | async-start | bytes 524288 | tf_op jit(solution)/shard_map/all_to_all | solution.py:14
  192.1 75.0 %all-to-all-start.5 = ((f32[32,64,256]{2,1,0:T(8,128)}), f32[32,64,256]{2,1,0:T(8,128)}, u32[]{:S(2)}, u32[]{:S(2)}) async-start(f32[32,64,256]{2,1,0:T(8,128)} %bitcast.93), calls=%async_computation.5 | async-start | bytes 4194304 | tf_op jit(solution)/shard_map/all_to_all | solution.py:14
  199.7 0.7 copy-start.2
  270.3 37.4 %all-to-all-start.6 = ((bf16[32,64,256]{2,1,0:T(8,128)(2,1)}), bf16[32,64,256]{2,1,0:T(8,128)(2,1)}, u32[]{:S(2)}, u32[]{:S(2)}) async-start(bf16[32,64,256]{2,1,0:T(8,128)(2,1)} %broadcast_in_dim.37), calls=%async_computation.6 | async-start | bytes 2097152 | tf_op jit(solution)/shard_map/all_to_all | solution.py:14
  280.4 56.5 %copy-start.3 = (bf16[128,256]{1,0:T(8,128)(2,1)}, bf16[128,256]{1,0:T(8,128)(2,1)S(1)}, u32[]{:S(2)}) copy-start(bf16[128,256]{1,0:T(8,128)(2,1)S(1)} %convolution_convert_fusion.1) | copy-start | bytes 196612
  310.2 25.6 %all-to-all-start.7 = ((bf16[16,128,128]{1,2,0:T(8,128)(2,1)}), bf16[16,128,128]{1,2,0:T(8,128)(2,1)S(1)}, u32[]{:S(2)}, u32[]{:S(2)}) async-start(bf16[16,128,128]{1,2,0:T(8,128)(2,1)} %fusion.7), calls=%async_computation.7 | async-start | bytes 1048576 | tf_op jit(solution)/shard_map/all_to_all | solution.py:14

commit v2 on v0

v2 whole, which is shorter than its diff:
```python
import math

import jax
import jax.numpy as jnp
from jax import lax
from jax.experimental import pallas as pl
from jax.experimental.pallas import tpu as pltpu
from jax.sharding import Mesh, PartitionSpec as P

decay_rate = 0.25
damping = 2.0
f4 = jnp.float32
bf = jnp.bfloat16
PANEL = 32

LAYER = ("x", "yhi", "core")
DP = ("ylo", "z")
YS, ZS = 4, 8

TN = (((0,), (0,)), ((), ()))
NN = (((1,), (0,)), ((), ()))
NT = (((1,), (1,)), ((), ()))


def exchange(parts, axis):
    return lax.all_to_all(parts, axis, split_axis=0, concat_axis=0, tiled=True)


def gather(part, axis, copies):
    return exchange(jnp.broadcast_to(part[None], (copies,) + part.shape), axis)


def call(body, outs, flops, name):
    return pl.pallas_call(
        body,
        out_shape=outs,
        name=name,
        cost_estimate=pl.CostEstimate(flops=flops, bytes_accessed=1 << 20, transcendentals=0),
        compiler_params=pltpu.CompilerParams(vmem_limit_bytes=40 << 20),
    )


def dot(a, b, dims):
    return lax.dot_general(a, b, dims, preferred_element_type=f4)


def split(v):
    hi = v.astype(bf)
    rest = v - hi.astype(f4)
    mid = rest.astype(bf)
    return hi, mid, (rest - mid.astype(f4)).astype(bf)


def exact_dot(a, b, dims):
    (ca,), (cb,) = dims[0]
    h, m, l = split(a)
    left = jnp.concatenate([h, h, m, m, h, l], axis=ca)
    h, m, l = split(b)
    right = jnp.concatenate([h, m, h, m, l, h], axis=cb)
    return dot(left, right, dims)


def project_kernel(acts_ref, factor_ref, basis_ref, parts_ref, moved_ref):
    zs, ys, rows, rank = basis_ref.shape
    projected = jnp.zeros((acts_ref.shape[0], rank), f4)
    moved = jnp.zeros((factor_ref.shape[0], rank), f4)
    for y in range(ys):
        for z in range(0, zs, 2):
            at = (y * zs + z) * rows
            block = jnp.concatenate([basis_ref[z, y], basis_ref[z + 1, y]], axis=0)
            projected += dot(acts_ref[:, at : at + 2 * rows], block, NN)
            moved += dot(factor_ref[:, at : at + 2 * rows], block, NN)
    moved_ref[...] = moved
    turned = projected.T.astype(bf)
    for j in range(ys * zs):
        parts_ref[j] = dot(turned, acts_ref[:, j * rows : (j + 1) * rows], NN).astype(bf)


def applied_kernel(parts_ref, moved_ref, applied_ref, rows_ref, gram_ref, *, share, scale):
    total = parts_ref[0].astype(f4)
    for j in range(1, parts_ref.shape[0]):
        total = total + parts_ref[j].astype(f4)
    applied = decay_rate * moved_ref[...] + share * total.T
    applied_ref[...] = applied
    rows_ref[...] = applied * scale
    gram_ref[...] = exact_dot(applied, applied, TN)


def cross_kernel(applied_ref, slab_ref, cross_ref):
    hi, lo, _ = split(applied_ref[...])
    both = jnp.concatenate([hi, lo], axis=0)
    n = slab_ref.shape[2]
    for j in range(slab_ref.shape[0]):
        twice = jnp.concatenate([slab_ref[j], slab_ref[j]], axis=0)
        cross_ref[j * n : (j + 1) * n] = dot(twice, both, TN)


def reciprocal(x):
    r = pl.reciprocal(x, approx=True)
    r = r * (2.0 - x * r)
    return r * (2.0 - x * r)


def invert_factor(ref):
    n = ref.shape[0]
    halves = n // 128
    lane = lax.broadcasted_iota(jnp.int32, (8, 128), 1)
    row = lax.broadcasted_iota(jnp.int32, (8, 128), 0)

    def read(r, count, q):
        return ref[r : r + count, q * 128 : (q + 1) * 128]

    def write(r, count, q, v):
        ref[r : r + count, q * 128 : (q + 1) * 128] = v

    def splat(v, i, j):
        return jnp.broadcast_to(v[j // 128][i : i + 1, j % 128 : j % 128 + 1], (8, 128))

    def lanes(v, j):
        return jnp.broadcast_to(v[j // 128][:, j % 128 : j % 128 + 1], (8, 128))

    def rows(v, i):
        return [jnp.broadcast_to(h[i : i + 1, :], (8, 128)) for h in v]

    steps = PANEL // 8
    for p0 in range(0, n, PANEL):
        slabs = [[read(p0 + 8 * s, 8, q) for q in range(halves)] for s in range(steps)]
        for s in range(steps):
            k0 = p0 + 8 * s
            v = slabs[s]
            d = [[splat(v, i, k0 + j) for j in range(i + 1)] for i in range(8)]
            low = [[None] * 8 for _ in range(8)]
            root = []
            for j in range(8):
                r = reciprocal(d[j][j])
                root.append(lax.rsqrt(d[j][j]))
                for i in range(j + 1, 8):
                    low[i][j] = d[i][j] * r
                for k in range(j + 1, 8):
                    for i in range(k, 8):
                        d[i][k] = d[i][k] - low[i][j] * d[k][j]
            w = [[None] * 8 for _ in range(8)]
            for j in range(8):
                for i in range(j + 1, 8):
                    t = low[i][j]
                    for m in range(j + 1, i):
                        t = t + low[i][m] * w[m][j]
                    w[i][j] = -t
            for i in range(8):
                for j in range(i):
                    w[i][j] = w[i][j] * root[i]
                w[i][i] = root[i]
            src = list(v)
            h = k0 // 128
            off = lane + (h * 128 - k0)
            inside = (off >= 0) & (off < 8)
            src[h] = jnp.where(inside, jnp.where(off == row, 1.0, 0.0), v[h])
            new = [jnp.zeros((8, 128), f4) for _ in range(halves)]
            for m in range(8):
                column = jnp.where(row >= m, w[m][m], 0.0)
                for i in range(m + 1, 8):
                    column = jnp.where(row >= i, w[i][m], column)
                source = rows(src, m)
                new = [new[q] + column * source[q] for q in range(halves)]
            slabs[s] = new
            for q in range(halves):
                write(k0, 8, q, new[q])
            spread = [rows(new, j) for j in range(8)] if s < steps - 1 else None
            for t in range(s + 1, steps):
                u = slabs[t]
                b = [lanes(u, k0 + m) for m in range(8)]
                cur = list(u)
                cur[h] = jnp.where(inside, 0.0, u[h])
                for j in range(8):
                    c = w[j][0] * b[0]
                    for m in range(1, j + 1):
                        c = c + w[j][m] * b[m]
                    cur = [cur[q] - c * spread[j][q] for q in range(halves)]
                slabs[t] = cur
        e0 = p0 + PANEL
        if e0 < n:
            top = jnp.concatenate([jnp.concatenate(v, axis=1) for v in slabs], axis=0)
            ahead = lax.broadcasted_iota(jnp.int32, (PANEL, n), 1) - p0
            below = lax.broadcasted_iota(jnp.int32, (PANEL, n), 0)
            kept = jnp.where((ahead > below) & (ahead < PANEL), 0.0, top)
            out = exact_dot(top, kept, TN)
            for q in range(halves):
                old = read(e0, n - e0, q)
                at = lax.broadcasted_iota(jnp.int32, (n - e0, 128), 1) + (q * 128 - p0)
                old = jnp.where((at >= 0) & (at < PANEL), 0.0, old)
                write(e0, n - e0, q, old - out[e0:, q * 128 : (q + 1) * 128])


def factor_kernel(gram_ref, applied_ref, inverse_ref, eigen_ref, fresh_ref):
    n = gram_ref.shape[0]
    inverse_ref[...] = gram_ref[...]
    invert_factor(inverse_ref)
    a = lax.broadcasted_iota(jnp.int32, (n, n), 0)
    b = lax.broadcasted_iota(jnp.int32, (n, n), 1)
    inverse = jnp.where(a >= b, inverse_ref[...], 0.0)
    inverse_ref[...] = inverse
    diagonal = jnp.sum(jnp.where(a == b, inverse, 0.0), axis=0, keepdims=True)
    eigen_ref[...] = (1.0 / diagonal).astype(bf)
    fresh_ref[...] = exact_dot(applied_ref[...], inverse, NT).astype(bf)


def scale_kernel(cross_ref, inverse_ref, eigen_ref, scaled_ref):
    total = cross_ref[0]
    for j in range(1, cross_ref.shape[0]):
        total = total + cross_ref[j]
    coupling = exact_dot(total, inverse_ref[...], NT)
    factors = 1.0 / (eigen_ref[...].astype(f4) + damping) - 1.0 / damping
    scaled = (coupling * factors).astype(bf)
    for j in range(scaled_ref.shape[0]):
        scaled_ref[j] = scaled


def result_kernel(fresh_ref, scaled_ref, slab_ref, out_ref):
    fresh = fresh_ref[...]
    for j in range(slab_ref.shape[0]):
        chunks = []
        for c in (2 * j, 2 * j + 1):
            chunks.append(scaled_ref[(c % YS) * ZS + c // YS])
        moved = dot(fresh, jnp.concatenate(chunks, axis=0), NT)
        out_ref[j] = (slab_ref[j].astype(f4) / damping + moved).astype(bf)


def per_device(acts, factor_old, basis_old, grads):
    token_rows, factor_rows = acts[0], factor_old[0]
    ranks = YS * ZS
    rows, rank = basis_old.shape[1:]
    width = factor_rows.shape[1]
    tokens = token_rows.shape[0] * ranks
    blocks, _, cols = grads.shape
    flops = 2 * width * rank * token_rows.shape[0]

    near = gather(basis_old[0], "ylo", YS)
    old_basis = lax.all_gather(near, "z", axis=0, tiled=False)
    slab = exchange(grads, LAYER)
    old_basis, slab = lax.optimization_barrier((old_basis, slab))
    parts, moved = call(
        project_kernel,
        (
            jax.ShapeDtypeStruct((ranks, rank, rows), bf),
            jax.ShapeDtypeStruct((rows, rank), f4),
        ),
        5 * flops // 2,
        "project",
    )(token_rows, factor_rows, old_basis)
    parts = exchange(parts, DP)

    def applied_body(*refs):
        applied_kernel(*refs, share=(1.0 - decay_rate) / tokens, scale=math.sqrt(width))

    applied, applied_rows, gram_local = call(
        applied_body,
        (
            jax.ShapeDtypeStruct((rows, rank), f4),
            jax.ShapeDtypeStruct((rows, rank), f4),
            jax.ShapeDtypeStruct((rank, rank), f4),
        ),
        flops // 4,
        "applied",
    )(parts, moved)
    gram_parts = exchange(gram_local.reshape(ranks, rank // ranks, rank), DP)
    gram = gather(jnp.sum(gram_parts, axis=0), DP, ranks).reshape(rank, rank)

    cross = call(
        cross_kernel,
        jax.ShapeDtypeStruct((blocks * cols, rank), f4),
        flops // 2,
        "cross",
    )(applied, slab)
    cross = lax.psum_scatter(cross, "z", scatter_dimension=0, tiled=True)
    inverse, eigen, fresh = call(
        factor_kernel,
        (
            jax.ShapeDtypeStruct((rank, rank), f4),
            jax.ShapeDtypeStruct((1, rank), bf),
            jax.ShapeDtypeStruct((rows, rank), bf),
        ),
        20 * flops,
        "factor",
    )(gram, applied)
    cross, inverse = lax.optimization_barrier((cross, inverse))
    cross = exchange(cross.reshape(YS, blocks * cols // ranks, rank), "ylo")
    scaled = call(
        scale_kernel,
        jax.ShapeDtypeStruct((ranks, blocks * cols // ranks, rank), bf),
        flops // 8,
        "scale",
    )(cross, inverse, eigen)
    scaled = exchange(scaled, DP)
    result = call(
        result_kernel,
        jax.ShapeDtypeStruct((blocks, rows, cols), bf),
        flops // 2,
        "result",
    )(fresh, scaled, slab)
    conditioned = exchange(result, LAYER)
    return (fresh[None], eigen, conditioned, applied_rows[None])


def solution(mesh):
    fine = Mesh(mesh.devices.reshape(4, 2, 2, YS, ZS), LAYER + DP)
    in_specs = (
        P(LAYER, DP, None),
        P(LAYER, DP, None),
        P(LAYER, DP, None),
        P(None, DP, LAYER),
    )
    out_specs = (
        P(LAYER, DP, None),
        P(LAYER, None),
        P(None, DP, LAYER),
        P(LAYER, DP, None),
    )
    return jax.shard_map(
        per_device, mesh=fine, in_specs=in_specs, out_specs=out_specs, check_vma=False
    )
```

time: 1080 us -> 259 us (0.24)
  the two profiles are of different devices: /device:TPU:1 before, /device:TPU:72 now
where the time goes in v2:
time: 259 us
  blocking collectives  198 us (76%)
  waiting for transfers between devices  24.2 us (9%)
  Pallas kernels  17.3 us (7%)
  between operations  14.1 us (5%)
  local copies, waits for them, and re-layouts  5.31 us (2%)
    all_to_all x8, blocking collectives, exchange(): return lax.all_to_all(parts, axis, split_axis=0, concat_axis=0, tiled=True)  198 us
    all_gather x1, waiting for transfers between devices, per_device(): old_basis = lax.all_gather(near, 'z', axis=0, tiled=False)  19.1 us
    pallas_call x1, Pallas kernels, per_device(): call(factor_kernel, (jax.ShapeDtypeStruct((rank, rank), f4), jax.ShapeDty...  10.8 us
  transfers between devices with their start and end apart: 2, of which 2 were waited for; matrix products, arithmetic and copies ran while one was open for 0% of the time, Pallas kernels for 4%

profile of v2, /device:TPU:72, one launch (start us, length us, event | category | flops | bytes accessed | tf_op | source)
XLA Modules:
  0.0 258.8 jit_solution(3906124452370332234)
XLA Ops:
  7.2 0.0 copy-start
  7.2 0.0 all-gather.3.cloned.1.call-start
  7.2 1.0 broadcast_in_dim.20
  8.2 12.3 %all_to_all.40 = bf16[4,128,256]{2,1,0:T(8,128)(2,1)} all-to-all(bf16[4,128,256]{2,1,0:T(8,128)(2,1)S(1)} %broadcast_in_dim.20), channel_id=1, replica_groups=mesh['x'=4,'yhi'=2,'core'=2,'ylo'=4,'z'=8] {'ylo'}, dimensions={0} | all-to-all | bytes 524288 | tf_op jit(solution)/shard_map/all_to_all | solution.py:26
  20.5 0.0 all-gather.3.cloned.1.call-update
  20.5 0.0 reduce-scatter.2.cloned.1.call-start
  20.6 28.6 %all_to_all.41.slab_ref = bf16[16,128,128]{2,1,0:T(8,128)(2,1)S(1)} all-to-all(bf16[16,128,128]{2,1,0:T(8,128)(2,1)} %param.7), channel_id=1, replica_groups=mesh['x'=4,'yhi'=2,'core'=2,'ylo'=4,'z'=8] {'x','yhi','core'}, dimensions={0} | all-to-all | bytes 1048576 | tf_op jit(solution)/shard_map/all_to_all | solution.py:26
  49.2 19.1 %all-gather.3.cloned.1.call-done = bf16[32,128,256]{2,1,0:T(8,128)(2,1)} async-done(((bf16[4,128,256]{2,1,0:T(8,128)(2,1)}), bf16[32,128,256]{2,1,0:T(8,128)(2,1)}) %all-gather.3.cloned.1.call-update) | async-done | bytes 2097168 | tf_op jit(solution)/shard_map/all_gather | solution.py:238
  68.3 0.0 copy-done
  68.3 0.0 copy-start.1
  68.3 1.6 copy-done.1
  69.9 0.0 copy-start.2
  69.9 1.2 copy-done.2
  71.1 2.8 %project.1 = (bf16[32,256,128]{2,1,0:T(8,128)(2,1)S(1)}, f32[128,256]{1,0:T(8,128)S(1)}) custom-call(bf16[256,4096]{1,0:T(8,128)(2,1)S(1)} %bitcast.9, bf16[128,4096]{1,0:T(8,128)(2,1)S(1)} %bitcast.11, bf16[8,4,128,256]{3,2,1,0:T(8,128)(2,1)S(1)} %bitcast.10), custom_call_target="tpu_custom_call" | custom-call | flops 1342177280 | bytes 1048576 | tf_op jit(solution)/shard_map/project/pallas_call | solution.py:241
  73.9 55.2 %all_to_all.42.refs_0_ = bf16[32,256,128]{2,1,0:T(8,128)(2,1)S(1)} all-to-all(bf16[32,256,128]{2,1,0:T(8,128)(2,1)S(1)} %get-tuple-element.17), channel_id=1, replica_groups=mesh['x'=4,'yhi'=2,'core'=2,'ylo'=4,'z'=8] {'ylo','z'}, dimensions={0} | all-to-all | bytes 4194304 | tf_op jit(solution)/shard_map/all_to_all | solution.py:26
  129.1 1.0 applied.1
  130.1 1.8 cross.1
  131.9 0.0 reduce-scatter.2.cloned.1.call-update
  132.0 16.2 %all_to_all.43 = f32[32,8,256]{2,1,0:T(8,128)S(1)} all-to-all(f32[32,8,256]{2,1,0:T(8,128)S(1)} %bitcast.12), channel_id=1, replica_groups=mesh['x'=4,'yhi'=2,'core'=2,'ylo'=4,'z'=8] {'ylo','z'}, dimensions={0} | all-to-all | bytes 524288 | tf_op jit(solution)/shard_map/all_to_all | solution.py:26
  148.3 16.2 %all_to_all.44 = f32[32,8,256]{2,1,0:T(8,128)S(1)} all-to-all(f32[32,8,256]{2,1,0:T(8,128)S(1)} %broadcast_in_dim.21), channel_id=1, replica_groups=mesh['x'=4,'yhi'=2,'core'=2,'ylo'=4,'z'=8] {'ylo','z'}, dimensions={0} | all-to-all | bytes 524288 | tf_op jit(solution)/shard_map/all_to_all | solution.py:26
  164.5 10.8 %factor.1 = (f32[256,256]{1,0:T(8,128)S(1)}, bf16[1,256]{1,0:T(2,128)(2,1)}, bf16[128,256]{1,0:T(8,128)(2,1)}) custom-call(f32[256,256]{1,0:T(8,128)S(1)} %bitcast.13, f32[128,256]{1,0:T(8,128)S(1)} %get-tuple-element.20.applied_ref), custom_call_target="tpu_custom_call" | custom-call | flops 10737418240 | bytes 1048576 | tf_op jit(solution)/shard_map/factor/pallas_call | solution.py:275
  175.2 5.0 %reduce-scatter.2.cloned.1.call-done = f32[256,256]{1,0:T(8,128)} async-done(((f32[2048,256]{1,0:T(8,128)}), f32[256,256]{1,0:T(8,128)}) %reduce-scatter.2.cloned.1.call-update) | async-done | bytes 262160 | tf_op jit(solution)/shard_map/reduce_scatter | solution.py:274
  180.3 0.0 copy-start.3
  180.3 11.5 %all_to_all.45.cross_ref = f32[4,64,256]{2,1,0:T(8,128)S(1)} all-to-all(f32[4,64,256]{2,1,0:T(8,128)} %bitcast.15), channel_id=1, replica_groups=mesh['x'=4,'yhi'=2,'core'=2,'ylo'=4,'z'=8] {'ylo'}, dimensions={0} | all-to-all | bytes 524288 | tf_op jit(solution)/shard_map/all_to_all | solution.py:26
  191.8 0.0 copy-start.4
  191.8 0.7 copy-done.4
  192.5 0.5 scale.1
  192.9 30.8 %all_to_all.46.scaled_ref = bf16[32,64,256]{2,1,0:T(8,128)(2,1)S(1)} all-to-all(bf16[32,64,256]{2,1,0:T(8,128)(2,1)S(1)} %scale.1), channel_id=1, replica_groups=mesh['x'=4,'yhi'=2,'core'=2,'ylo'=4,'z'=8] {'ylo','z'}, dimensions={0} | all-to-all | bytes 2097152 | tf_op jit(solution)/shard_map/all_to_all | solution.py:26
  223.8 0.0 copy-done.3
  223.8 0.4 result.1
  224.2 26.9 %all_to_all.47 = bf16[16,128,128]{2,1,0:T(8,128)(2,1)S(1)} all-to-all(bf16[16,128,128]{2,1,0:T(8,128)(2,1)S(1)} %result.1), channel_id=1, replica_groups=mesh['x'=4,'yhi'=2,'core'=2,'ylo'=4,'z'=8] {'x','yhi','core'}, dimensions={0} | all-to-all | bytes 1048576 | tf_op jit(solution)/shard_map/all_to_all | solution.py:26
  251.2 0.8 copy.9
  (2 shorter events, 0.1 us)
Async XLA Ops:
  7.2 61.1 %copy-start = (bf16[1,256,4096]{2,1,0:T(8,128)(2,1)S(1)}, bf16[1,256,4096]{2,1,0:T(8,128)(2,1)}, u32[]{:S(2)}) copy-start(bf16[1,256,4096]{2,1,0:T(8,128)(2,1)} %param.4) | copy-start | bytes 6291460
  7.2 61.1 %all-gather.3.cloned.1.call-start = ((), (), s32[]{:S(2)}) async-start(), calls=%async_computation.10 | async-start | bytes 2359296 | tf_op jit(solution)/shard_map/all_gather | solution.py:238
  20.5 159.7 %reduce-scatter.2.cloned.1.call-start = ((), (), s32[]{:S(2)}) async-start(), calls=%async_computation.9 | async-start | bytes 2359296 | tf_op jit(solution)/shard_map/reduce_scatter | solution.py:274
  68.3 1.6 copy-start.1
  69.9 1.2 copy-start.2
  180.3 43.5 %copy-start.3 = (bf16[128,256]{1,0:T(8,128)(2,1)S(1)}, bf16[128,256]{1,0:T(8,128)(2,1)}, u32[]{:S(2)}) copy-start(bf16[128,256]{1,0:T(8,128)(2,1)} %get-tuple-element.21.fresh_ref) | copy-start | bytes 196612
  191.8 0.7 copy-start.4
Sparse Core Ops, SparseCore 0:
  20.7 47.6 all-gather.2
  132.1 48.1 reduce-scatter.1

commit v3 on v2

--- a/solution.py
+++ b/solution.py
@@ -30,13 +30,14 @@
     return exchange(jnp.broadcast_to(part[None], (copies,) + part.shape), axis)
 
 
-def call(body, outs, flops, name):
+def call(body, outs, flops, name, **more):
     return pl.pallas_call(
         body,
         out_shape=outs,
+        **more,
         name=name,
         cost_estimate=pl.CostEstimate(flops=flops, bytes_accessed=1 << 20, transcendentals=0),
-        compiler_params=pltpu.CompilerParams(vmem_limit_bytes=40 << 20),
+        compiler_params=pltpu.CompilerParams(vmem_limit_bytes=24 << 20),
     )
 
 
@@ -60,39 +61,75 @@
     return dot(left, right, dims)
 
 
-def project_kernel(acts_ref, factor_ref, basis_ref, parts_ref, moved_ref):
+def project_kernel(acts_ref, basis_ref, parts_ref):
     zs, ys, rows, rank = basis_ref.shape
-    projected = jnp.zeros((acts_ref.shape[0], rank), f4)
-    moved = jnp.zeros((factor_ref.shape[0], rank), f4)
+    turned = basis_product(acts_ref, basis_ref).T.astype(bf)
+    for j in range(ys * zs):
+        parts_ref[j] = dot(turned, acts_ref[:, j * rows : (j + 1) * rows], NN).astype(bf)
+
+
+def basis_product(left_ref, basis_ref):
+    zs, ys, rows, rank = basis_ref.shape
+    total = jnp.zeros((left_ref.shape[0], rank), f4)
     for y in range(ys):
         for z in range(0, zs, 2):
             at = (y * zs + z) * rows
             block = jnp.concatenate([basis_ref[z, y], basis_ref[z + 1, y]], axis=0)
-            projected += dot(acts_ref[:, at : at + 2 * rows], block, NN)
-            moved += dot(factor_ref[:, at : at + 2 * rows], block, NN)
-    moved_ref[...] = moved
-    turned = projected.T.astype(bf)
-    for j in range(ys * zs):
-        parts_ref[j] = dot(turned, acts_ref[:, j * rows : (j + 1) * rows], NN).astype(bf)
-
-
-def applied_kernel(parts_ref, moved_ref, applied_ref, rows_ref, gram_ref, *, share, scale):
+            total += dot(left_ref[:, at : at + 2 * rows], block, NN)
+    return total
+
+
+def applied_kernel(parts_ref, factor_ref, basis_ref, applied_ref, rows_ref, *, share, scale):
     total = parts_ref[0].astype(f4)
     for j in range(1, parts_ref.shape[0]):
         total = total + parts_ref[j].astype(f4)
-    applied = decay_rate * moved_ref[...] + share * total.T
-    applied_ref[...] = applied
+    applied = decay_rate * basis_product(factor_ref, basis_ref) + share * total.T
+    applied_ref[...] = jnp.broadcast_to(applied[None], applied_ref.shape)
     rows_ref[...] = applied * scale
+
+
+def turn_kernel(grads_ref, turned_ref):
+    blocks, quarter = grads_ref.shape[0], turned_ref.shape[1]
+    share = grads_ref.shape[2] // quarter
+    for b in range(blocks):
+        turned = grads_ref[b].astype(f4).T.astype(bf)
+        for q in range(share):
+            turned_ref[b * share + q] = turned[q * quarter : (q + 1) * quarter]
+
+
+def turn_back_kernel(turned_ref, out_ref):
+    blocks, quarter = out_ref.shape[0], turned_ref.shape[1]
+    share = out_ref.shape[2] // quarter
+    for b in range(blocks):
+        block = jnp.concatenate([turned_ref[b * share + q] for q in range(share)], axis=0)
+        out_ref[b] = block.astype(f4).T.astype(bf)
+
+
+def slab_of(slab_ref, y, ys):
+    return jnp.concatenate([slab_ref[j] for j in range(y, slab_ref.shape[0], ys)], axis=0)
+
+
+def cross_kernel(applied_ref, slab_ref, cross_ref):
+    ys = applied_ref.shape[0]
+    total = jnp.zeros(cross_ref.shape, f4)
+    for y in range(ys):
+        hi, lo, _ = split(applied_ref[y])
+        slab = slab_of(slab_ref, y, ys)
+        twice = jnp.concatenate([slab, slab], axis=1)
+        total += dot(twice, jnp.concatenate([hi, lo], axis=0), NN)
+    cross_ref[...] = total
+
+
+def gram_kernel(applied_ref, gram_ref):
+    applied = jnp.concatenate([applied_ref[j] for j in range(applied_ref.shape[0])], axis=0)
     gram_ref[...] = exact_dot(applied, applied, TN)
 
 
-def cross_kernel(applied_ref, slab_ref, cross_ref):
-    hi, lo, _ = split(applied_ref[...])
-    both = jnp.concatenate([hi, lo], axis=0)
-    n = slab_ref.shape[2]
-    for j in range(slab_ref.shape[0]):
-        twice = jnp.concatenate([slab_ref[j], slab_ref[j]], axis=0)
-        cross_ref[j * n : (j + 1) * n] = dot(twice, both, TN)
+def sum_kernel(parts_ref, total_ref):
+    total = parts_ref[0]
+    for j in range(1, parts_ref.shape[0]):
+        total = total + parts_ref[j]
+    total_ref[...] = jnp.broadcast_to(total[None], total_ref.shape)
 
 
 def reciprocal(x):
@@ -191,7 +228,7 @@
                 write(e0, n - e0, q, old - out[e0:, q * 128 : (q + 1) * 128])
 
 
-def factor_kernel(gram_ref, applied_ref, inverse_ref, eigen_ref, fresh_ref):
+def factor_kernel(gram_ref, inverse_ref, eigen_ref, scale_ref):
     n = gram_ref.shape[0]
     inverse_ref[...] = gram_ref[...]
     invert_factor(inverse_ref)
@@ -200,29 +237,32 @@
     inverse = jnp.where(a >= b, inverse_ref[...], 0.0)
     inverse_ref[...] = inverse
     diagonal = jnp.sum(jnp.where(a == b, inverse, 0.0), axis=0, keepdims=True)
-    eigen_ref[...] = (1.0 / diagonal).astype(bf)
-    fresh_ref[...] = exact_dot(applied_ref[...], inverse, NT).astype(bf)
-
-
-def scale_kernel(cross_ref, inverse_ref, eigen_ref, scaled_ref):
-    total = cross_ref[0]
-    for j in range(1, cross_ref.shape[0]):
-        total = total + cross_ref[j]
-    coupling = exact_dot(total, inverse_ref[...], NT)
-    factors = 1.0 / (eigen_ref[...].astype(f4) + damping) - 1.0 / damping
-    scaled = (coupling * factors).astype(bf)
+    eigen = (1.0 / diagonal).astype(bf)
+    eigen_ref[...] = eigen
+    scale_ref[...] = 1.0 / (eigen.astype(f4) + damping) - 1.0 / damping
+
+
+def fresh_kernel(place_ref, applied_ref, inverse_ref, fresh_ref, own_ref):
+    for y in range(applied_ref.shape[0]):
+        fresh_ref[y] = exact_dot(applied_ref[y], inverse_ref[...], NT).astype(bf)
+    own_ref[...] = fresh_ref[place_ref[0]]
+
+
+def scale_kernel(cross_ref, inverse_ref, scale_ref, scaled_ref):
+    coupling = exact_dot(cross_ref[...], inverse_ref[...], NT)
+    scaled = (coupling * scale_ref[...]).astype(bf)
     for j in range(scaled_ref.shape[0]):
         scaled_ref[j] = scaled
 
 
 def result_kernel(fresh_ref, scaled_ref, slab_ref, out_ref):
-    fresh = fresh_ref[...]
-    for j in range(slab_ref.shape[0]):
-        chunks = []
-        for c in (2 * j, 2 * j + 1):
-            chunks.append(scaled_ref[(c % YS) * ZS + c // YS])
-        moved = dot(fresh, jnp.concatenate(chunks, axis=0), NT)
-        out_ref[j] = (slab_ref[j].astype(f4) / damping + moved).astype(bf)
+    ys, quarter = fresh_ref.shape[0], slab_ref.shape[1]
+    scaled = jnp.concatenate([scaled_ref[j] for j in range(scaled_ref.shape[0])], axis=0)
+    for y in range(ys):
+        moved = dot(scaled, fresh_ref[y], NT)
+        result = (slab_of(slab_ref, y, ys).astype(f4) / damping + moved).astype(bf)
+        for j in range(out_ref.shape[0] // ys):
+            out_ref[j * ys + y] = result[j * quarter : (j + 1) * quarter]
 
 
 def per_device(acts, factor_old, basis_old, grads):
@@ -234,70 +274,88 @@
     blocks, _, cols = grads.shape
     flops = 2 * width * rank * token_rows.shape[0]
 
+    wide_columns = blocks * cols // YS
+    chunk = wide_columns // ZS
+    blocked = jax.ShapeDtypeStruct((blocks * YS, cols // YS, rows), bf)
+
     near = gather(basis_old[0], "ylo", YS)
     old_basis = lax.all_gather(near, "z", axis=0, tiled=False)
-    slab = exchange(grads, LAYER)
+    slab = exchange(call(turn_kernel, blocked, flops // 64, "turn")(grads), LAYER + ("ylo",))
     old_basis, slab = lax.optimization_barrier((old_basis, slab))
-    parts, moved = call(
+    parts = call(
         project_kernel,
+        jax.ShapeDtypeStruct((ranks, rank, rows), bf),
+        2 * flops,
+        "project",
+    )(token_rows, old_basis)
+    parts = exchange(parts, DP)
+
+    def applied_body(*refs):
+        applied_kernel(*refs, share=(1.0 - decay_rate) / tokens, scale=math.sqrt(width))
+
+    applied, applied_rows = call(
+        applied_body,
         (
-            jax.ShapeDtypeStruct((ranks, rank, rows), bf),
+            jax.ShapeDtypeStruct((YS, rows, rank), f4),
             jax.ShapeDtypeStruct((rows, rank), f4),
         ),
-        5 * flops // 2,
-        "project",
-    )(token_rows, factor_rows, old_basis)
-    parts = exchange(parts, DP)
-
-    def applied_body(*refs):
-        applied_kernel(*refs, share=(1.0 - decay_rate) / tokens, scale=math.sqrt(width))
-
-    applied, applied_rows, gram_local = call(
-        applied_body,
+        flops // 2,
+        "applied",
+    )(parts, factor_rows, old_basis)
+    applied = exchange(applied, "ylo")
+    cross = call(
+        cross_kernel, jax.ShapeDtypeStruct((wide_columns, rank), f4), flops // 2, "cross"
+    )(applied, slab)
+    cross, applied = lax.optimization_barrier((cross, applied))
+    cross = lax.psum_scatter(cross, "z", scatter_dimension=0, tiled=True)
+    gram = call(gram_kernel, jax.ShapeDtypeStruct((rank, rank), f4), flops, "gram")(applied)
+    factor_out = (
+        jax.ShapeDtypeStruct((rank, rank), f4),
+        jax.ShapeDtypeStruct((1, rank), bf),
+        jax.ShapeDtypeStruct((1, rank), f4),
+    )
+
+    def factored(gram):
+        parts = exchange(gram.reshape(ZS, rank // ZS, rank), "z")
+        total = call(
+            sum_kernel, jax.ShapeDtypeStruct((ZS, rank // ZS, rank), f4), flops // 64, "sum"
+        )(parts)
+        total = exchange(total, "z").reshape(rank, rank)
+        return call(factor_kernel, factor_out, 20 * flops, "factor")(total)
+
+    inverse, eigen, scale = lax.cond(
+        lax.axis_index("z") < ZS,
+        factored,
+        lambda _: tuple(jnp.zeros(v.shape, v.dtype) for v in factor_out),
+        gram,
+    )
+    place = lax.axis_index("ylo").astype(jnp.int32).reshape(1)
+    vmem, smem = pl.BlockSpec(memory_space=pltpu.VMEM), pl.BlockSpec(memory_space=pltpu.SMEM)
+    wide_fresh, fresh = call(
+        fresh_kernel,
         (
-            jax.ShapeDtypeStruct((rows, rank), f4),
-            jax.ShapeDtypeStruct((rows, rank), f4),
-            jax.ShapeDtypeStruct((rank, rank), f4),
-        ),
-        flops // 4,
-        "applied",
-    )(parts, moved)
-    gram_parts = exchange(gram_local.reshape(ranks, rank // ranks, rank), DP)
-    gram = gather(jnp.sum(gram_parts, axis=0), DP, ranks).reshape(rank, rank)
-
-    cross = call(
-        cross_kernel,
-        jax.ShapeDtypeStruct((blocks * cols, rank), f4),
-        flops // 2,
-        "cross",
-    )(applied, slab)
-    cross = lax.psum_scatter(cross, "z", scatter_dimension=0, tiled=True)
-    inverse, eigen, fresh = call(
-        factor_kernel,
-        (
-            jax.ShapeDtypeStruct((rank, rank), f4),
-            jax.ShapeDtypeStruct((1, rank), bf),
+            jax.ShapeDtypeStruct((YS, rows, rank), bf),
             jax.ShapeDtypeStruct((rows, rank), bf),
         ),
-        20 * flops,
-        "factor",
-    )(gram, applied)
-    cross, inverse = lax.optimization_barrier((cross, inverse))
-    cross = exchange(cross.reshape(YS, blocks * cols // ranks, rank), "ylo")
+        2 * flops,
+        "fresh",
+        in_specs=[smem, vmem, vmem],
+    )(place, applied, inverse)
     scaled = call(
         scale_kernel,
-        jax.ShapeDtypeStruct((ranks, blocks * cols // ranks, rank), bf),
+        jax.ShapeDtypeStruct((ZS, chunk, rank), bf),
         flops // 8,
         "scale",
-    )(cross, inverse, eigen)
-    scaled = exchange(scaled, DP)
-    result = call(
-        result_kernel,
+    )(cross, inverse, scale)
+    scaled = exchange(scaled, "z")
+    result = call(result_kernel, blocked, flops // 2, "result")(wide_fresh, scaled, slab)
+    result = exchange(result, LAYER + ("ylo",))
+    conditioned = call(
+        turn_back_kernel,
         jax.ShapeDtypeStruct((blocks, rows, cols), bf),
-        flops // 2,
-        "result",
-    )(fresh, scaled, slab)
-    conditioned = exchange(result, LAYER)
+        flops // 64,
+        "turn_back",
+    )(result)
     return (fresh[None], eigen, conditioned, applied_rows[None])
 
 

time: 259 us -> 241 us (0.931)
  the two profiles are of different devices: /device:TPU:72 before, /device:TPU:1 now
where the time goes in v3:
time: 241 us
  blocking collectives  175 us (73%)
  waiting for transfers between devices  23 us (10%)
  Pallas kernels  21 us (9%)
  between operations  14.1 us (6%)
  local copies, waits for them, and re-layouts  4.48 us (2%)
  starting transfers between devices  3.65 us (2%)
    all_to_all x7, blocking collectives, exchange(): return lax.all_to_all(parts, axis, split_axis=0, concat_axis=0, tiled=True)  175 us
    all_gather x1, waiting for transfers between devices, per_device(): old_basis = lax.all_gather(near, 'z', axis=0, tiled=False)  15.4 us
    pallas_call x1, Pallas kernels, factored(): return call(factor_kernel, factor_out, 20 * flops, 'factor')(total)  10.2 us
    all_to_all x1, waiting for transfers between devices, exchange(): return lax.all_to_all(parts, axis, split_axis=0, concat_axis=0, tiled=True)  7.56 us
  transfers between devices with their start and end apart: 3, of which 2 were waited for; matrix products, arithmetic and copies ran while one was open for 0% of the time, Pallas kernels for 5%

profile of v3, /device:TPU:1, one launch (start us, length us, event | category | flops | bytes accessed | tf_op | source)
XLA Modules:
  0.0 240.8 jit_solution(9721634333015948723)
XLA Ops:
  7.2 0.0 copy-start.2
  7.2 0.0 all-gather.3.cloned.1.call-start
  7.2 1.0 broadcast_in_dim.14
  8.2 11.3 %all_to_all.40 = bf16[4,128,256]{2,1,0:T(8,128)(2,1)} all-to-all(bf16[4,128,256]{2,1,0:T(8,128)(2,1)S(1)} %broadcast_in_dim.14), channel_id=1, replica_groups=mesh['x'=4,'yhi'=2,'core'=2,'ylo'=4,'z'=8] {'ylo'}, dimensions={0} | all-to-all | bytes 524288 | tf_op jit(solution)/shard_map/all_to_all | solution.py:26
  19.5 0.0 all-gather.3.cloned.1.call-update
  19.6 0.0 reduce-scatter.2.cloned.1.call-start
  19.6 0.0 copy-start.4
  19.6 1.0 copy-done.4
  20.6 0.2 turn.1
  20.9 30.4 %all_to_all.41.slab_ref = bf16[64,32,128]{2,1,0:T(8,128)(2,1)S(1)} all-to-all(bf16[64,32,128]{2,1,0:T(8,128)(2,1)S(1)} %turn.1), channel_id=1, replica_groups=mesh['x'=4,'yhi'=2,'core'=2,'ylo'=4,'z'=8] {'x','yhi','core','ylo'}, dimensions={0} | all-to-all | bytes 1048576 | tf_op jit(solution)/shard_map/all_to_all | solution.py:26
  51.3 15.4 %all-gather.3.cloned.1.call-done = bf16[32,128,256]{2,1,0:T(8,128)(2,1)} async-done(((bf16[4,128,256]{2,1,0:T(8,128)(2,1)}), bf16[32,128,256]{2,1,0:T(8,128)(2,1)}) %all-gather.3.cloned.1.call-update) | async-done | bytes 2097168 | tf_op jit(solution)/shard_map/all_gather | solution.py:282
  66.7 0.0 copy-done.2
  66.7 0.0 copy-start
  66.7 1.6 copy-done
  68.3 3.0 %project.1 = bf16[32,256,128]{2,1,0:T(8,128)(2,1)S(1)} custom-call(bf16[256,4096]{1,0:T(8,128)(2,1)S(1)} %bitcast.11, bf16[8,4,128,256]{3,2,1,0:T(8,128)(2,1)S(1)} %bitcast.9), custom_call_target="tpu_custom_call" | custom-call | flops 1073741824 | bytes 1048576 | tf_op jit(solution)/shard_map/project/pallas_call | solution.py:285
  71.3 0.0 copy-start.1
  71.3 0.0 copy-start.3
  71.3 53.7 %all_to_all.42.refs_0_ = bf16[32,256,128]{2,1,0:T(8,128)(2,1)S(1)} all-to-all(bf16[32,256,128]{2,1,0:T(8,128)(2,1)S(1)} %project.1), channel_id=1, replica_groups=mesh['x'=4,'yhi'=2,'core'=2,'ylo'=4,'z'=8] {'ylo','z'}, dimensions={0} | all-to-all | bytes 4194304 | tf_op jit(solution)/shard_map/all_to_all | solution.py:26
  125.0 0.0 copy-done.1
  125.0 0.0 copy-done.3
  125.0 1.3 applied.1
  126.3 20.0 %all_to_all.43.applied_ref = f32[4,128,256]{2,1,0:T(8,128)S(1)} all-to-all(f32[4,128,256]{2,1,0:T(8,128)S(1)} %get-tuple-element.17), channel_id=1, replica_groups=mesh['x'=4,'yhi'=2,'core'=2,'ylo'=4,'z'=8] {'ylo'}, dimensions={0} | all-to-all | bytes 1048576 | tf_op jit(solution)/shard_map/all_to_all | solution.py:26
  146.3 1.2 cross.1
  147.5 0.0 reduce-scatter.2.cloned.1.call-update
  147.5 0.6 gram.1
  148.2 37.3 %conditional.1 = ((f32[256,256]{1,0:T(8,128)S(1)}, bf16[1,256]{1,0:T(2,128)(2,1)}, f32[1,256]{1,0:T(1,128)S(1)})) conditional(s32[]{:T(128)} %convert_element_type.3, () %tuple.19, f32[256,256]{1,0:T(8,128)S(1)} %gram.1), branch_computations={%region_0.0_spmd, %region_1.0_spmd} | conditional | flops 10745806848 | bytes 3145736 | solution.py:326
  148.2 14.1 %all_to_all.38.parts_ref = f32[8,32,256]{2,1,0:T(8,128)S(1)} all-to-all(f32[8,32,256]{2,1,0:T(8,128)S(1)} %bitcast.14), channel_id=1, replica_groups=mesh['x'=4,'yhi'=2,'core'=2,'ylo'=4,'z'=8] {'z'}, dimensions={0} | all-to-all | bytes 524288 | tf_op jit(solution)/shard_map/cond/branch_1_fun/all_to_all | solution.py:26
  162.3 13.0 %all_to_all.39 = f32[8,32,256]{2,1,0:T(8,128)S(1)} all-to-all(f32[8,32,256]{2,1,0:T(8,128)S(1)} %sum.1), channel_id=1, replica_groups=mesh['x'=4,'yhi'=2,'core'=2,'ylo'=4,'z'=8] {'z'}, dimensions={0} | all-to-all | bytes 524288 | tf_op jit(solution)/shard_map/cond/branch_1_fun/all_to_all | solution.py:26
  175.3 10.2 %factor.1 = (f32[256,256]{1,0:T(8,128)S(1)}, bf16[1,256]{1,0:T(2,128)(2,1)}, f32[1,256]{1,0:T(1,128)S(1)}) custom-call(f32[256,256]{1,0:T(8,128)S(1)} %bitcast.13), custom_call_target="tpu_custom_call" | custom-call | flops 10737418240 | bytes 1048576 | tf_op jit(solution)/shard_map/cond/branch_1_fun/factor/pallas_call | solution.py:324
  185.5 0.0 reduce-scatter.2.cloned.1.call-done.cross_ref
  185.5 0.0 copy-start.5
  185.5 0.8 copy-done.5
  186.4 1.1 scale.1
  187.4 3.6 %all-to-all-start.6 = ((bf16[8,64,256]{2,1,0:T(8,128)(2,1)}), bf16[8,64,256]{2,1,0:T(8,128)(2,1)S(1)}, u32[]{:S(2)}, u32[]{:S(2)}) async-start(bf16[8,64,256]{2,1,0:T(8,128)(2,1)} %scale.1), calls=%async_computation.7 | async-start | bytes 524288 | tf_op jit(solution)/shard_map/all_to_all | solution.py:26
  191.0 1.8 fresh.1
  192.8 7.6 %all-to-all-done.6.scaled_ref = bf16[8,64,256]{2,1,0:T(8,128)(2,1)S(1)} async-done(((bf16[8,64,256]{2,1,0:T(8,128)(2,1)}), bf16[8,64,256]{2,1,0:T(8,128)(2,1)S(1)}, u32[]{:S(2)}, u32[]{:S(2)}) %all-to-all-start.6) | async-done | bytes 262176 | tf_op jit(solution)/shard_map/all_to_all | solution.py:26
  200.3 0.4 result.1
  200.8 32.2 %all_to_all.44.turned_ref = bf16[64,32,128]{2,1,0:T(8,128)(2,1)S(1)} all-to-all(bf16[64,32,128]{2,1,0:T(8,128)(2,1)S(1)} %result.1), channel_id=1, replica_groups=mesh['x'=4,'yhi'=2,'core'=2,'ylo'=4,'z'=8] {'x','yhi','core','ylo'}, dimensions={0} | all-to-all | bytes 1048576 | tf_op jit(solution)/shard_map/all_to_all | solution.py:26
  233.0 1.0 turn_back.1
  (1 shorter events, 0.0 us)
Async XLA Ops:
  7.2 59.5 %copy-start.2 = (bf16[1,256,4096]{2,1,0:T(8,128)(2,1)S(1)}, bf16[1,256,4096]{2,1,0:T(8,128)(2,1)}, u32[]{:S(2)}) copy-start(bf16[1,256,4096]{2,1,0:T(8,128)(2,1)} %param.6) | copy-start | bytes 6291460
  7.2 59.5 %all-gather.3.cloned.1.call-start = ((), (), s32[]{:S(2)}) async-start(), calls=%async_computation.10 | async-start | bytes 2359296 | tf_op jit(solution)/shard_map/all_gather | solution.py:282
  19.6 166.0 %reduce-scatter.2.cloned.1.call-start = ((), (), s32[]{:S(2)}) async-start(), calls=%async_computation.9 | async-start | bytes 589824 | tf_op jit(solution)/shard_map/reduce_scatter | solution.py:310
  19.6 1.0 copy-start.4
  66.7 1.6 copy-start
  71.3 53.7 %copy-start.1 = (bf16[32,128,256]{2,1,0:T(8,128)(2,1)S(1)}, bf16[32,128,256]{2,1,0:T(8,128)(2,1)}, u32[]{:S(2)}) copy-start(bf16[32,128,256]{2,1,0:T(8,128)(2,1)} %all-gather.3.cloned.1.call-done) | copy-start | bytes 6291460
  71.3 53.7 %copy-start.3 = (bf16[1,128,4096]{2,1,0:T(8,128)(2,1)S(1)}, bf16[1,128,4096]{2,1,0:T(8,128)(2,1)}, u32[]{:S(2)}) copy-start(bf16[1,128,4096]{2,1,0:T(8,128)(2,1)} %param.7) | copy-start | bytes 3145732
  185.5 0.8 copy-start.5
  187.4 12.9 %all-to-all-start.6 = ((bf16[8,64,256]{2,1,0:T(8,128)(2,1)}), bf16[8,64,256]{2,1,0:T(8,128)(2,1)S(1)}, u32[]{:S(2)}, u32[]{:S(2)}) async-start(bf16[8,64,256]{2,1,0:T(8,128)(2,1)} %scale.1), calls=%async_computation.7 | async-start | bytes 524288 | tf_op jit(solution)/shard_map/all_to_all | solution.py:26
Sparse Core Ops, SparseCore 0:
  19.7 46.9 all-gather.2
  147.7 36.0 reduce-scatter.1

commit v4 on v3

--- a/solution.py
+++ b/solution.py
@@ -14,7 +14,8 @@
 PANEL = 32
 
 LAYER = ("x", "yhi", "core")
-DP = ("ylo", "z")
+Y = ("ypair", "yside")
+DP = Y + ("z",)
 YS, ZS = 4, 8
 
 TN = (((0,), (0,)), ((), ()))
@@ -61,11 +62,35 @@
     return dot(left, right, dims)
 
 
-def project_kernel(acts_ref, basis_ref, parts_ref):
-    zs, ys, rows, rank = basis_ref.shape
-    turned = basis_product(acts_ref, basis_ref).T.astype(bf)
-    for j in range(ys * zs):
-        parts_ref[j] = dot(turned, acts_ref[:, j * rows : (j + 1) * rows], NN).astype(bf)
+def columns(ref, pair, side, quarter, first=0, count=None):
+    at = (2 * pair + side) * quarter + first
+    return ref[:, pl.ds(pl.multiple_of(at, 128), count or quarter)]
+
+
+def deal_kernel(place_ref, acts_ref, out_ref):
+    quarter = out_ref.shape[1] // 2
+    for pair in range(2):
+        out_ref[:, pair * quarter : (pair + 1) * quarter] = columns(
+            acts_ref, pair, 1 - place_ref[0], quarter
+        )
+
+
+def project_kernel(acts_ref, basis_ref, turned_ref):
+    turned_ref[...] = basis_product(acts_ref, basis_ref).T.astype(bf)
+
+
+def token_kernel(place_ref, turned_ref, other_ref, acts_ref, got_ref, parts_ref):
+    parts, _, rows = parts_ref.shape
+    zs = parts // 2
+    quarter = zs * rows
+    for pair in range(2):
+        for z in range(0, zs, 2):
+            own = columns(acts_ref, pair, place_ref[0], quarter, z * rows, 2 * rows)
+            at = pair * quarter + z * rows
+            both = dot(turned_ref[...], own, NN)
+            both += dot(other_ref[...], got_ref[:, at : at + 2 * rows], NN)
+            parts_ref[pair * zs + z] = both[:, :rows].astype(bf)
+            parts_ref[pair * zs + z + 1] = both[:, rows:].astype(bf)
 
 
 def basis_product(left_ref, basis_ref):
@@ -110,14 +135,17 @@
 
 
 def cross_kernel(applied_ref, slab_ref, cross_ref):
-    ys = applied_ref.shape[0]
-    total = jnp.zeros(cross_ref.shape, f4)
-    for y in range(ys):
-        hi, lo, _ = split(applied_ref[y])
-        slab = slab_of(slab_ref, y, ys)
-        twice = jnp.concatenate([slab, slab], axis=1)
-        total += dot(twice, jnp.concatenate([hi, lo], axis=0), NN)
-    cross_ref[...] = total
+    ys, quarter = applied_ref.shape[0], slab_ref.shape[1]
+    split_rows = [split(applied_ref[y]) for y in range(ys)]
+    both = jnp.concatenate([v[0] for v in split_rows] + [v[1] for v in split_rows], axis=0)
+    group = 4
+    for j in range(0, slab_ref.shape[0] // ys, group):
+        blocks = []
+        for y in range(ys):
+            held = [slab_ref[i * ys + y] for i in range(j, j + group)]
+            blocks.append(jnp.concatenate(held, axis=0))
+        left = jnp.concatenate(blocks + blocks, axis=1)
+        cross_ref[j * quarter : (j + group) * quarter] = dot(left, both, NN)
 
 
 def gram_kernel(applied_ref, gram_ref):
@@ -278,17 +306,43 @@
     chunk = wide_columns // ZS
     blocked = jax.ShapeDtypeStruct((blocks * YS, cols // YS, rows), bf)
 
-    near = gather(basis_old[0], "ylo", YS)
+    near = gather(basis_old[0], Y, YS)
     old_basis = lax.all_gather(near, "z", axis=0, tiled=False)
-    slab = exchange(call(turn_kernel, blocked, flops // 64, "turn")(grads), LAYER + ("ylo",))
-    old_basis, slab = lax.optimization_barrier((old_basis, slab))
+    place = lax.axis_index(Y).astype(jnp.int32).reshape(1)
+    vmem, smem = pl.BlockSpec(memory_space=pltpu.VMEM), pl.BlockSpec(memory_space=pltpu.SMEM)
+    side = lax.axis_index("yside").astype(jnp.int32).reshape(1)
+
+    def swap(part):
+        return lax.ppermute(part, "yside", [(0, 1), (1, 0)])
+
+    tokens_here = token_rows.shape[0]
+    got = swap(
+        call(
+            deal_kernel,
+            jax.ShapeDtypeStruct((tokens_here, width // 2), bf),
+            flops // 64,
+            "deal",
+            in_specs=[smem, vmem],
+        )(side, token_rows)
+    )
+    slab = lax.cond(
+        lax.axis_index("z") < ZS,
+        lambda v: exchange(call(turn_kernel, blocked, flops // 64, "turn")(v), LAYER + Y),
+        lambda _: jnp.zeros(blocked.shape, bf),
+        grads,
+    )
+    old_basis, slab, got = lax.optimization_barrier((old_basis, slab, got))
+    turned = call(
+        project_kernel, jax.ShapeDtypeStruct((rank, tokens_here), bf), flops, "project"
+    )(token_rows, old_basis)
     parts = call(
-        project_kernel,
-        jax.ShapeDtypeStruct((ranks, rank, rows), bf),
-        2 * flops,
-        "project",
-    )(token_rows, old_basis)
-    parts = exchange(parts, DP)
+        token_kernel,
+        jax.ShapeDtypeStruct((ranks // 2, rank, rows), bf),
+        flops,
+        "tokens",
+        in_specs=[smem] + [vmem] * 4,
+    )(side, turned, swap(turned), token_rows, got)
+    parts = exchange(parts, ("ypair", "z"))
 
     def applied_body(*refs):
         applied_kernel(*refs, share=(1.0 - decay_rate) / tokens, scale=math.sqrt(width))
@@ -302,7 +356,7 @@
         flops // 2,
         "applied",
     )(parts, factor_rows, old_basis)
-    applied = exchange(applied, "ylo")
+    applied = exchange(applied, Y)
     cross = call(
         cross_kernel, jax.ShapeDtypeStruct((wide_columns, rank), f4), flops // 2, "cross"
     )(applied, slab)
@@ -329,8 +383,6 @@
         lambda _: tuple(jnp.zeros(v.shape, v.dtype) for v in factor_out),
         gram,
     )
-    place = lax.axis_index("ylo").astype(jnp.int32).reshape(1)
-    vmem, smem = pl.BlockSpec(memory_space=pltpu.VMEM), pl.BlockSpec(memory_space=pltpu.SMEM)
     wide_fresh, fresh = call(
         fresh_kernel,
         (
@@ -341,6 +393,7 @@
         "fresh",
         in_specs=[smem, vmem, vmem],
     )(place, applied, inverse)
+    cross, wide_fresh = lax.optimization_barrier((cross, wide_fresh))
     scaled = call(
         scale_kernel,
         jax.ShapeDtypeStruct((ZS, chunk, rank), bf),
@@ -349,7 +402,7 @@
     )(cross, inverse, scale)
     scaled = exchange(scaled, "z")
     result = call(result_kernel, blocked, flops // 2, "result")(wide_fresh, scaled, slab)
-    result = exchange(result, LAYER + ("ylo",))
+    result = exchange(result, LAYER + Y)
     conditioned = call(
         turn_back_kernel,
         jax.ShapeDtypeStruct((blocks, rows, cols), bf),
@@ -360,7 +413,7 @@
 
 
 def solution(mesh):
-    fine = Mesh(mesh.devices.reshape(4, 2, 2, YS, ZS), LAYER + DP)
+    fine = Mesh(mesh.devices.reshape(4, 2, 2, YS // 2, 2, ZS), LAYER + DP)
     in_specs = (
         P(LAYER, DP, None),
         P(LAYER, DP, None),

time: 241 us -> 227 us (0.942)
  waiting for transfers between devices: 23 us -> 2.69 us
  blocking collectives: 175 us -> 178 us
  starting transfers between devices: 3.65 us -> 6.29 us
    all_gather x1, waiting for transfers between devices: 15.4 us -> 0.3 us  [per_device(): old_basis = lax.all_gather(near, 'z', axis=0, tiled=False)]
    all_to_all x1 -> x0, waiting for transfers between devices: 7.56 us -> none  [exchange(): return lax.all_to_all(parts, axis, split_axis=0, concat_axis=0, tiled=True)]
    ppermute x0 -> x2, starting transfers between devices: none -> 6.21 us  [swap(): return lax.ppermute(part, 'yside', [(0, 1), (1, 0)])]
    all_to_all x1 -> x0, starting transfers between devices: 3.57 us -> none  [exchange(): return lax.all_to_all(parts, axis, split_axis=0, concat_axis=0, tiled=True)]
    all_to_all x7 -> x8, blocking collectives: 175 us -> 178 us  [exchange(): return lax.all_to_all(parts, axis, split_axis=0, concat_axis=0, tiled=True)]
  transfers between devices with their start and end apart: 3 -> 4, of which waited for: 2 -> 2; matrix products, arithmetic and copies ran while one was open for 0% -> 0% of each run, Pallas kernels for 5% -> 7%
where the time goes in v4:
time: 227 us
  blocking collectives  178 us (78%)
  Pallas kernels  20.6 us (9%)
  between operations  14.1 us (6%)
  starting transfers between devices  6.29 us (3%)
  local copies, waits for them, and re-layouts  4.89 us (2%)
  waiting for transfers between devices  2.69 us (1%)
    all_to_all x8, blocking collectives, exchange(): return lax.all_to_all(parts, axis, split_axis=0, concat_axis=0, tiled=True)  178 us
    pallas_call x1, Pallas kernels, factored(): return call(factor_kernel, factor_out, 20 * flops, 'factor')(total)  10.2 us
    ppermute x2, starting transfers between devices, swap(): return lax.ppermute(part, 'yside', [(0, 1), (1, 0)])  6.21 us
  transfers between devices with their start and end apart: 4, of which 2 were waited for; matrix products, arithmetic and copies ran while one was open for 0% of the time, Pallas kernels for 7%

profile of v4, /device:TPU:1, one launch (start us, length us, event | category | flops | bytes accessed | tf_op | source)
XLA Modules:
  0.0 226.8 jit_solution(14942896756376772198)
XLA Ops:
  7.2 0.0 all-gather.3.cloned.1.call-start
  7.2 0.9 broadcast_in_dim.14
  8.1 11.3 %all_to_all.40 = bf16[4,128,256]{2,1,0:T(8,128)(2,1)} all-to-all(bf16[4,128,256]{2,1,0:T(8,128)(2,1)S(1)} %broadcast_in_dim.14), channel_id=1, replica_groups=mesh['x'=4,'yhi'=2,'core'=2,'ypair'=2,'yside'=2,'z'=8] {'ypair','yside'}, dimensions={0} | all-to-all | bytes 524288 | tf_op jit(solution)/shard_map/all_to_all | solution.py:27
  19.4 0.0 all-gather.3.cloned.1.call-update
  19.4 0.0 reduce-scatter.2.cloned.1.call-start
  19.5 0.0 copy-start
  19.5 1.6 copy-done
  21.1 1.0 deal.1
  22.1 0.0 copy-start.1
  22.1 2.9 %collective-permute-start = (bf16[256,2048]{1,0:T(8,128)(2,1)}, bf16[256,2048]{1,0:T(8,128)(2,1)S(1)}, u32[]{:S(2)}, u32[]{:S(2)}) collective-permute-start(bf16[256,2048]{1,0:T(8,128)(2,1)} %deal.1), channel_id=1, source_target_pairs={{0,8},{8,0},{1,9},{9,1},{2,10},{10,2},{3,11},{11,3},{4,12},{12,4},... | collective-permute-start | bytes 3145736 | tf_op jit(solution)/shard_map/ppermute | solution.py:316
  24.9 41.3 %conditional.2 = (bf16[64,32,128]{2,1,0:T(8,128)(2,1)}) conditional(s32[]{:T(128)} %convert_element_type.4, () %tuple.24, (bf16[16,128,128]{2,1,0:T(8,128)(2,1)}) %tuple.30), branch_computations={%region_0.0_spmd, %region_1.0_spmd} | conditional | flops 8388608 | bytes 2097160 | solution.py:328
  25.0 1.2 turn.1
  26.2 40.0 %all_to_all.37 = bf16[64,32,128]{2,1,0:T(8,128)(2,1)} all-to-all(bf16[64,32,128]{2,1,0:T(8,128)(2,1)S(1)} %turn.1), channel_id=1, replica_groups=mesh['x'=4,'yhi'=2,'core'=2,'ypair'=2,'yside'=2,'z'=8] {'x','yhi','core'..., dimensions={0} | all-to-all | bytes 1048576 | tf_op jit(solution)/shard_map/cond/branch_1_fun/all_to_all | solution.py:27
  66.2 0.0 collective-permute-done.got_ref
  66.2 0.3 all-gather.3.cloned.1.call-done
  66.5 0.0 copy-done.1
  66.5 0.0 copy-start.2
  66.5 1.6 copy-done.2
  68.1 0.8 project.1.turned_ref
  68.9 3.4 %collective-permute-start.1 = (bf16[256,256]{1,0:T(8,128)(2,1)S(1)}, bf16[256,256]{1,0:T(8,128)(2,1)S(1)}, u32[]{:S(2)}, u32[]{:S(2)}) collective-permute-start(bf16[256,256]{1,0:T(8,128)(2,1)S(1)} %project.1.turned_ref), channel_id=1, source_target_pairs={{0,8},{8,0},{1,9},{9,1},{2,10},{10,2},{3,11},{11,3},{4,12},{12,4},... | collective-permute-start | bytes 393224 | tf_op jit(solution)/shard_map/ppermute | solution.py:316
  72.3 2.3 %collective-permute-done.1.other_ref = bf16[256,256]{1,0:T(8,128)(2,1)S(1)} collective-permute-done((bf16[256,256]{1,0:T(8,128)(2,1)S(1)}, bf16[256,256]{1,0:T(8,128)(2,1)S(1)}, u32[]{:S(2)}, u32[]{:S(2)}) %collective-permute-start.1) | collective-permute-done | bytes 131104 | tf_op jit(solution)/shard_map/ppermute | solution.py:316
  74.6 0.7 tokens.1
  75.3 0.0 copy-start.3
  75.3 43.6 %all_to_all.41.refs_0_ = bf16[16,256,128]{2,1,0:T(8,128)(2,1)S(1)} all-to-all(bf16[16,256,128]{2,1,0:T(8,128)(2,1)S(1)} %tokens.1), channel_id=1, replica_groups=mesh['x'=4,'yhi'=2,'core'=2,'ypair'=2,'yside'=2,'z'=8] {'ypair','z'}, dimensions={0} | all-to-all | bytes 2097152 | tf_op jit(solution)/shard_map/all_to_all | solution.py:27
  118.9 0.0 copy-done.3
  118.9 0.0 copy-start.5
  118.9 1.2 applied.1
  120.1 16.4 %all_to_all.42.applied_ref = f32[4,128,256]{2,1,0:T(8,128)S(1)} all-to-all(f32[4,128,256]{2,1,0:T(8,128)S(1)} %get-tuple-element.25), channel_id=1, replica_groups=mesh['x'=4,'yhi'=2,'core'=2,'ypair'=2,'yside'=2,'z'=8] {'ypair','yside'}, dimensions={0} | all-to-all | bytes 1048576 | tf_op jit(solution)/shard_map/all_to_all | solution.py:27
  136.5 0.0 copy-done.5
  136.5 1.2 cross.1
  137.7 0.0 reduce-scatter.2.cloned.1.call-update
  137.8 0.6 gram.1
  138.4 37.5 %conditional.3 = ((f32[256,256]{1,0:T(8,128)S(1)}, bf16[1,256]{1,0:T(2,128)(2,1)}, f32[1,256]{1,0:T(1,128)S(1)})) conditional(s32[]{:T(128)} %convert_element_type.4, () %tuple.27, f32[256,256]{1,0:T(8,128)S(1)} %gram.1), branch_computations={%region_2.0_spmd, %region_3.0_spmd} | conditional | flops 10745806848 | bytes 3145736 | solution.py:380
  138.4 14.1 %all_to_all.38.parts_ref = f32[8,32,256]{2,1,0:T(8,128)S(1)} all-to-all(f32[8,32,256]{2,1,0:T(8,128)S(1)} %bitcast.17), channel_id=1, replica_groups=mesh['x'=4,'yhi'=2,'core'=2,'ypair'=2,'yside'=2,'z'=8] {'z'}, dimensions={0} | all-to-all | bytes 524288 | tf_op jit(solution)/shard_map/cond/branch_1_fun/all_to_all | solution.py:27
  152.5 13.1 %all_to_all.39 = f32[8,32,256]{2,1,0:T(8,128)S(1)} all-to-all(f32[8,32,256]{2,1,0:T(8,128)S(1)} %sum.1), channel_id=1, replica_groups=mesh['x'=4,'yhi'=2,'core'=2,'ypair'=2,'yside'=2,'z'=8] {'z'}, dimensions={0} | all-to-all | bytes 524288 | tf_op jit(solution)/shard_map/cond/branch_1_fun/all_to_all | solution.py:27
  165.6 10.2 %factor.1 = (f32[256,256]{1,0:T(8,128)S(1)}, bf16[1,256]{1,0:T(2,128)(2,1)}, f32[1,256]{1,0:T(1,128)S(1)}) custom-call(f32[256,256]{1,0:T(8,128)S(1)} %bitcast.16), custom_call_target="tpu_custom_call" | custom-call | flops 10737418240 | bytes 1048576 | tf_op jit(solution)/shard_map/cond/branch_1_fun/factor/pallas_call | solution.py:378
  175.8 1.8 fresh.1
  177.6 0.0 reduce-scatter.2.cloned.1.call-done.cross_ref
  177.6 0.0 copy-start.4
  177.6 0.8 copy-done.4
  178.5 0.4 scale.1
  178.8 11.7 %all_to_all.43.scaled_ref = bf16[8,64,256]{2,1,0:T(8,128)(2,1)S(1)} all-to-all(bf16[8,64,256]{2,1,0:T(8,128)(2,1)S(1)} %scale.1), channel_id=1, replica_groups=mesh['x'=4,'yhi'=2,'core'=2,'ypair'=2,'yside'=2,'z'=8] {'z'}, dimensions={0} | all-to-all | bytes 524288 | tf_op jit(solution)/shard_map/all_to_all | solution.py:27
  190.6 0.4 result.1
  191.0 27.9 %all_to_all.44.turned_ref = bf16[64,32,128]{2,1,0:T(8,128)(2,1)S(1)} all-to-all(bf16[64,32,128]{2,1,0:T(8,128)(2,1)S(1)} %result.1), channel_id=1, replica_groups=mesh['x'=4,'yhi'=2,'core'=2,'ypair'=2,'yside'=2,'z'=8] {'x','yhi','core'..., dimensions={0} | all-to-all | bytes 1048576 | tf_op jit(solution)/shard_map/all_to_all | solution.py:27
  218.9 1.0 turn_back.1
  (1 shorter events, 0.0 us)
Async XLA Ops:
  7.2 59.4 %all-gather.3.cloned.1.call-start = ((), (), s32[]{:S(2)}) async-start(), calls=%async_computation.10 | async-start | bytes 2359296 | tf_op jit(solution)/shard_map/all_gather | solution.py:310
  19.4 158.2 %reduce-scatter.2.cloned.1.call-start = ((), (), s32[]{:S(2)}) async-start(), calls=%async_computation.9 | async-start | bytes 589824 | tf_op jit(solution)/shard_map/reduce_scatter | solution.py:364
  19.5 1.6 copy-start
  22.1 44.5 %copy-start.1 = (bf16[1,256,4096]{2,1,0:T(8,128)(2,1)S(1)}, bf16[1,256,4096]{2,1,0:T(8,128)(2,1)}, u32[]{:S(2)}) copy-start(bf16[1,256,4096]{2,1,0:T(8,128)(2,1)} %param.8) | copy-start | bytes 6291460
  22.1 44.1 %collective-permute-start = (bf16[256,2048]{1,0:T(8,128)(2,1)}, bf16[256,2048]{1,0:T(8,128)(2,1)S(1)}, u32[]{:S(2)}, u32[]{:S(2)}) collective-permute-start(bf16[256,2048]{1,0:T(8,128)(2,1)} %deal.1), channel_id=1, source_target_pairs={{0,8},{8,0},{1,9},{9,1},{2,10},{10,2},{3,11},{11,3},{4,12},{12,4},... | collective-permute-start | bytes 3145736 | tf_op jit(solution)/shard_map/ppermute | solution.py:316
  66.5 1.6 copy-start.2
  68.9 5.7 %collective-permute-start.1 = (bf16[256,256]{1,0:T(8,128)(2,1)S(1)}, bf16[256,256]{1,0:T(8,128)(2,1)S(1)}, u32[]{:S(2)}, u32[]{:S(2)}) collective-permute-start(bf16[256,256]{1,0:T(8,128)(2,1)S(1)} %project.1.turned_ref), channel_id=1, source_target_pairs={{0,8},{8,0},{1,9},{9,1},{2,10},{10,2},{3,11},{11,3},{4,12},{12,4},... | collective-permute-start | bytes 393224 | tf_op jit(solution)/shard_map/ppermute | solution.py:316
  75.3 43.6 %copy-start.3 = (bf16[1,128,4096]{2,1,0:T(8,128)(2,1)S(1)}, bf16[1,128,4096]{2,1,0:T(8,128)(2,1)}, u32[]{:S(2)}) copy-start(bf16[1,128,4096]{2,1,0:T(8,128)(2,1)} %param.9) | copy-start | bytes 3145732
  118.9 17.6 %copy-start.5 = (bf16[64,32,128]{2,1,0:T(8,128)(2,1)S(1)}, bf16[64,32,128]{2,1,0:T(8,128)(2,1)}, u32[]{:S(2)}) copy-start(bf16[64,32,128]{2,1,0:T(8,128)(2,1)} %get-tuple-element.45.slab_ref) | copy-start | bytes 1572868
  177.6 0.8 copy-start.4
Sparse Core Ops, SparseCore 0:
  19.5 46.9 all-gather.2
  137.9 32.5 reduce-scatter.1

commit v5 on v4

--- a/solution.py
+++ b/solution.py
@@ -104,11 +104,15 @@
     return total
 
 
-def applied_kernel(parts_ref, factor_ref, basis_ref, applied_ref, rows_ref, *, share, scale):
+def moved_kernel(factor_ref, basis_ref, moved_ref):
+    moved_ref[...] = decay_rate * basis_product(factor_ref, basis_ref)
+
+
+def applied_kernel(parts_ref, moved_ref, applied_ref, rows_ref, *, share, scale):
     total = parts_ref[0].astype(f4)
     for j in range(1, parts_ref.shape[0]):
         total = total + parts_ref[j].astype(f4)
-    applied = decay_rate * basis_product(factor_ref, basis_ref) + share * total.T
+    applied = moved_ref[...] + share * total.T
     applied_ref[...] = jnp.broadcast_to(applied[None], applied_ref.shape)
     rows_ref[...] = applied * scale
 
@@ -335,13 +339,19 @@
     turned = call(
         project_kernel, jax.ShapeDtypeStruct((rank, tokens_here), bf), flops, "project"
     )(token_rows, old_basis)
+    turned, old_basis = lax.optimization_barrier((turned, old_basis))
+    moved = call(
+        moved_kernel, jax.ShapeDtypeStruct((rows, rank), f4), flops // 2, "moved"
+    )(factor_rows, old_basis)
+    other = swap(turned)
+    other, moved = lax.optimization_barrier((other, moved))
     parts = call(
         token_kernel,
         jax.ShapeDtypeStruct((ranks // 2, rank, rows), bf),
         flops,
         "tokens",
         in_specs=[smem] + [vmem] * 4,
-    )(side, turned, swap(turned), token_rows, got)
+    )(side, turned, other, token_rows, got)
     parts = exchange(parts, ("ypair", "z"))
 
     def applied_body(*refs):
@@ -355,7 +365,7 @@
         ),
         flops // 2,
         "applied",
-    )(parts, factor_rows, old_basis)
+    )(parts, moved)
     applied = exchange(applied, Y)
     cross = call(
         cross_kernel, jax.ShapeDtypeStruct((wide_columns, rank), f4), flops // 2, "cross"

time: 227 us -> 227 us (level)
  no operation moved by 1% of the time
where the time goes in v5:
time: 227 us; the launch traced here: 226 us
  blocking collectives  178 us (78%)
  Pallas kernels  20.8 us (9%)
  between operations  14.1 us (6%)
  starting transfers between devices  6.29 us (3%)
  local copies, waits for them, and re-layouts  4.89 us (2%)
    all_to_all x8, blocking collectives, exchange(): return lax.all_to_all(parts, axis, split_axis=0, concat_axis=0, tiled=True)  178 us
    pallas_call x1, Pallas kernels, factored(): return call(factor_kernel, factor_out, 20 * flops, 'factor')(total)  10.2 us
    ppermute x2, starting transfers between devices, swap(): return lax.ppermute(part, 'yside', [(0, 1), (1, 0)])  6.21 us
  transfers between devices with their start and end apart: 4, of which 2 were waited for; matrix products, arithmetic and copies ran while one was open for 0% of the time, Pallas kernels for 7%

profile of v5, /device:TPU:1, one launch (start us, length us, event | category | flops | bytes accessed | tf_op | source)
XLA Modules:
  0.0 226.5 jit_solution(12641273583714233129)
XLA Ops:
  7.2 0.0 all-gather.3.cloned.1.call-start
  7.2 0.9 broadcast_in_dim.14
  8.1 11.3 %all_to_all.40 = bf16[4,128,256]{2,1,0:T(8,128)(2,1)} all-to-all(bf16[4,128,256]{2,1,0:T(8,128)(2,1)S(1)} %broadcast_in_dim.14), channel_id=1, replica_groups=mesh['x'=4,'yhi'=2,'core'=2,'ypair'=2,'yside'=2,'z'=8] {'ypair','yside'}, dimensions={0} | all-to-all | bytes 524288 | tf_op jit(solution)/shard_map/all_to_all | solution.py:27
  19.4 0.0 all-gather.3.cloned.1.call-update
  19.4 0.0 reduce-scatter.2.cloned.1.call-start
  19.5 0.0 copy-start
  19.5 1.6 copy-done
  21.1 1.0 deal.1
  22.1 0.0 copy-start.1
  22.1 2.9 %collective-permute-start = (bf16[256,2048]{1,0:T(8,128)(2,1)}, bf16[256,2048]{1,0:T(8,128)(2,1)S(1)}, u32[]{:S(2)}, u32[]{:S(2)}) collective-permute-start(bf16[256,2048]{1,0:T(8,128)(2,1)} %deal.1), channel_id=1, source_target_pairs={{0,8},{8,0},{1,9},{9,1},{2,10},{10,2},{3,11},{11,3},{4,12},{12,4},... | collective-permute-start | bytes 3145736 | tf_op jit(solution)/shard_map/ppermute | solution.py:320
  24.9 41.3 %conditional.2 = (bf16[64,32,128]{2,1,0:T(8,128)(2,1)}) conditional(s32[]{:T(128)} %convert_element_type.4, () %tuple.26, (bf16[16,128,128]{2,1,0:T(8,128)(2,1)}) %tuple.34), branch_computations={%region_0.0_spmd, %region_1.0_spmd} | conditional | flops 8388608 | bytes 2097160 | solution.py:332
  25.0 1.2 turn.1
  26.2 40.0 %all_to_all.37 = bf16[64,32,128]{2,1,0:T(8,128)(2,1)} all-to-all(bf16[64,32,128]{2,1,0:T(8,128)(2,1)S(1)} %turn.1), channel_id=1, replica_groups=mesh['x'=4,'yhi'=2,'core'=2,'ypair'=2,'yside'=2,'z'=8] {'x','yhi','core'..., dimensions={0} | all-to-all | bytes 1048576 | tf_op jit(solution)/shard_map/cond/branch_1_fun/all_to_all | solution.py:27
  66.2 0.0 collective-permute-done.got_ref
  66.2 0.3 all-gather.3.cloned.1.call-done
  66.5 0.0 copy-done.1
  66.5 0.0 copy-start.2
  66.5 1.6 copy-done.2
  68.1 0.0 copy-start.3
  68.1 0.8 project.1.turned_ref
  68.9 3.4 %collective-permute-start.1 = (bf16[256,256]{1,0:T(8,128)(2,1)S(1)}, bf16[256,256]{1,0:T(8,128)(2,1)S(1)}, u32[]{:S(2)}, u32[]{:S(2)}) collective-permute-start(bf16[256,256]{1,0:T(8,128)(2,1)S(1)} %project.1.turned_ref), channel_id=1, source_target_pairs={{0,8},{8,0},{1,9},{9,1},{2,10},{10,2},{3,11},{11,3},{4,12},{12,4},... | collective-permute-start | bytes 393224 | tf_op jit(solution)/shard_map/ppermute | solution.py:320
  72.3 0.0 copy-done.3
  72.3 0.4 moved.1.refs_1_
  72.7 1.9 collective-permute-done.1.other_ref
  74.6 0.7 tokens.1
  75.3 0.0 copy-start.5
  75.3 43.6 %all_to_all.41.refs_0_ = bf16[16,256,128]{2,1,0:T(8,128)(2,1)S(1)} all-to-all(bf16[16,256,128]{2,1,0:T(8,128)(2,1)S(1)} %tokens.1), channel_id=1, replica_groups=mesh['x'=4,'yhi'=2,'core'=2,'ypair'=2,'yside'=2,'z'=8] {'ypair','z'}, dimensions={0} | all-to-all | bytes 2097152 | tf_op jit(solution)/shard_map/all_to_all | solution.py:27
  118.9 0.9 applied.1
  119.8 16.4 %all_to_all.42.applied_ref = f32[4,128,256]{2,1,0:T(8,128)S(1)} all-to-all(f32[4,128,256]{2,1,0:T(8,128)S(1)} %get-tuple-element.33), channel_id=1, replica_groups=mesh['x'=4,'yhi'=2,'core'=2,'ypair'=2,'yside'=2,'z'=8] {'ypair','yside'}, dimensions={0} | all-to-all | bytes 1048576 | tf_op jit(solution)/shard_map/all_to_all | solution.py:27
  136.2 0.0 copy-done.5
  136.2 1.2 cross.1
  137.4 0.0 reduce-scatter.2.cloned.1.call-update
  137.5 0.6 gram.1
  138.1 37.6 %conditional.3 = ((f32[256,256]{1,0:T(8,128)S(1)}, bf16[1,256]{1,0:T(2,128)(2,1)}, f32[1,256]{1,0:T(1,128)S(1)})) conditional(s32[]{:T(128)} %convert_element_type.4, () %tuple.31, f32[256,256]{1,0:T(8,128)S(1)} %gram.1), branch_computations={%region_2.0_spmd, %region_3.0_spmd} | conditional | flops 10745806848 | bytes 3145736 | solution.py:390
  138.1 14.1 %all_to_all.38.parts_ref = f32[8,32,256]{2,1,0:T(8,128)S(1)} all-to-all(f32[8,32,256]{2,1,0:T(8,128)S(1)} %bitcast.17), channel_id=1, replica_groups=mesh['x'=4,'yhi'=2,'core'=2,'ypair'=2,'yside'=2,'z'=8] {'z'}, dimensions={0} | all-to-all | bytes 524288 | tf_op jit(solution)/shard_map/cond/branch_1_fun/all_to_all | solution.py:27
  152.2 13.2 %all_to_all.39 = f32[8,32,256]{2,1,0:T(8,128)S(1)} all-to-all(f32[8,32,256]{2,1,0:T(8,128)S(1)} %sum.1), channel_id=1, replica_groups=mesh['x'=4,'yhi'=2,'core'=2,'ypair'=2,'yside'=2,'z'=8] {'z'}, dimensions={0} | all-to-all | bytes 524288 | tf_op jit(solution)/shard_map/cond/branch_1_fun/all_to_all | solution.py:27
  165.4 10.2 %factor.1 = (f32[256,256]{1,0:T(8,128)S(1)}, bf16[1,256]{1,0:T(2,128)(2,1)}, f32[1,256]{1,0:T(1,128)S(1)}) custom-call(f32[256,256]{1,0:T(8,128)S(1)} %bitcast.16), custom_call_target="tpu_custom_call" | custom-call | flops 10737418240 | bytes 1048576 | tf_op jit(solution)/shard_map/cond/branch_1_fun/factor/pallas_call | solution.py:388
  175.7 1.8 fresh.1
  177.5 0.0 reduce-scatter.2.cloned.1.call-done.cross_ref
  177.5 0.0 copy-start.4
  177.5 0.8 copy-done.4
  178.3 0.4 scale.1
  178.7 11.9 %all_to_all.43.scaled_ref = bf16[8,64,256]{2,1,0:T(8,128)(2,1)S(1)} all-to-all(bf16[8,64,256]{2,1,0:T(8,128)(2,1)S(1)} %scale.1), channel_id=1, replica_groups=mesh['x'=4,'yhi'=2,'core'=2,'ypair'=2,'yside'=2,'z'=8] {'z'}, dimensions={0} | all-to-all | bytes 524288 | tf_op jit(solution)/shard_map/all_to_all | solution.py:27
  190.5 0.4 result.1
  191.0 27.6 %all_to_all.44.turned_ref = bf16[64,32,128]{2,1,0:T(8,128)(2,1)S(1)} all-to-all(bf16[64,32,128]{2,1,0:T(8,128)(2,1)S(1)} %result.1), channel_id=1, replica_groups=mesh['x'=4,'yhi'=2,'core'=2,'ypair'=2,'yside'=2,'z'=8] {'x','yhi','core'..., dimensions={0} | all-to-all | bytes 1048576 | tf_op jit(solution)/shard_map/all_to_all | solution.py:27
  218.6 1.0 turn_back.1
  (1 shorter events, 0.0 us)
Async XLA Ops:
  7.2 59.4 %all-gather.3.cloned.1.call-start = ((), (), s32[]{:S(2)}) async-start(), calls=%async_computation.10 | async-start | bytes 2359296 | tf_op jit(solution)/shard_map/all_gather | solution.py:314
  19.4 158.1 %reduce-scatter.2.cloned.1.call-start = ((), (), s32[]{:S(2)}) async-start(), calls=%async_computation.9 | async-start | bytes 589824 | tf_op jit(solution)/shard_map/reduce_scatter | solution.py:374
  19.5 1.6 copy-start
  22.1 44.5 %copy-start.1 = (bf16[1,256,4096]{2,1,0:T(8,128)(2,1)S(1)}, bf16[1,256,4096]{2,1,0:T(8,128)(2,1)}, u32[]{:S(2)}) copy-start(bf16[1,256,4096]{2,1,0:T(8,128)(2,1)} %param.8) | copy-start | bytes 6291460
  22.1 44.1 %collective-permute-start = (bf16[256,2048]{1,0:T(8,128)(2,1)}, bf16[256,2048]{1,0:T(8,128)(2,1)S(1)}, u32[]{:S(2)}, u32[]{:S(2)}) collective-permute-start(bf16[256,2048]{1,0:T(8,128)(2,1)} %deal.1), channel_id=1, source_target_pairs={{0,8},{8,0},{1,9},{9,1},{2,10},{10,2},{3,11},{11,3},{4,12},{12,4},... | collective-permute-start | bytes 3145736 | tf_op jit(solution)/shard_map/ppermute | solution.py:320
  66.5 1.6 copy-start.2
  68.1 4.1 %copy-start.3 = (bf16[1,128,4096]{2,1,0:T(8,128)(2,1)S(1)}, bf16[1,128,4096]{2,1,0:T(8,128)(2,1)}, u32[]{:S(2)}) copy-start(bf16[1,128,4096]{2,1,0:T(8,128)(2,1)} %param.9) | copy-start | bytes 3145732
  68.9 5.7 %collective-permute-start.1 = (bf16[256,256]{1,0:T(8,128)(2,1)S(1)}, bf16[256,256]{1,0:T(8,128)(2,1)S(1)}, u32[]{:S(2)}, u32[]{:S(2)}) collective-permute-start(bf16[256,256]{1,0:T(8,128)(2,1)S(1)} %project.1.turned_ref), channel_id=1, source_target_pairs={{0,8},{8,0},{1,9},{9,1},{2,10},{10,2},{3,11},{11,3},{4,12},{12,4},... | collective-permute-start | bytes 393224 | tf_op jit(solution)/shard_map/ppermute | solution.py:320
  75.3 60.9 %copy-start.5 = (bf16[64,32,128]{2,1,0:T(8,128)(2,1)S(1)}, bf16[64,32,128]{2,1,0:T(8,128)(2,1)}, u32[]{:S(2)}) copy-start(bf16[64,32,128]{2,1,0:T(8,128)(2,1)} %get-tuple-element.53.slab_ref) | copy-start | bytes 1572868
  177.5 0.8 copy-start.4
Sparse Core Ops, SparseCore 0:
  19.5 46.9 all-gather.2
  137.6 32.7 reduce-scatter.1

commit v6 on v5

--- a/solution.py
+++ b/solution.py
@@ -275,8 +275,11 @@
 
 
 def fresh_kernel(place_ref, applied_ref, inverse_ref, fresh_ref, own_ref):
-    for y in range(applied_ref.shape[0]):
-        fresh_ref[y] = exact_dot(applied_ref[y], inverse_ref[...], NT).astype(bf)
+    ys, rows, _ = applied_ref.shape
+    applied = jnp.concatenate([applied_ref[y] for y in range(ys)], axis=0)
+    fresh = exact_dot(applied, inverse_ref[...], NT).astype(bf)
+    for y in range(ys):
+        fresh_ref[y] = fresh[y * rows : (y + 1) * rows]
     own_ref[...] = fresh_ref[place_ref[0]]
 
 

time: 227 us -> 227 us (level)
  no operation moved by 1% of the time
where the time goes in v6:
time: 227 us; the launch traced here: 226 us
  blocking collectives  179 us (79%)
  Pallas kernels  20.3 us (9%)
  between operations  14.1 us (6%)
  starting transfers between devices  6.29 us (3%)
  local copies, waits for them, and re-layouts  4.89 us (2%)
    all_to_all x8, blocking collectives, exchange(): return lax.all_to_all(parts, axis, split_axis=0, concat_axis=0, tiled=True)  179 us
    pallas_call x1, Pallas kernels, factored(): return call(factor_kernel, factor_out, 20 * flops, 'factor')(total)  10.2 us
    ppermute x2, starting transfers between devices, swap(): return lax.ppermute(part, 'yside', [(0, 1), (1, 0)])  6.21 us
  transfers between devices with their start and end apart: 4, of which 2 were waited for; matrix products, arithmetic and copies ran while one was open for 0% of the time, Pallas kernels for 7%

profile of v6, /device:TPU:1, one launch (start us, length us, event | category | flops | bytes accessed | tf_op | source)
XLA Modules:
  0.0 226.5 jit_solution(256554006094682123)
XLA Ops:
  7.2 0.0 all-gather.3.cloned.1.call-start
  7.2 0.9 broadcast_in_dim.14
  8.1 11.3 %all_to_all.40 = bf16[4,128,256]{2,1,0:T(8,128)(2,1)} all-to-all(bf16[4,128,256]{2,1,0:T(8,128)(2,1)S(1)} %broadcast_in_dim.14), channel_id=1, replica_groups=mesh['x'=4,'yhi'=2,'core'=2,'ypair'=2,'yside'=2,'z'=8] {'ypair','yside'}, dimensions={0} | all-to-all | bytes 524288 | tf_op jit(solution)/shard_map/all_to_all | solution.py:27
  19.4 0.0 all-gather.3.cloned.1.call-update
  19.4 0.0 reduce-scatter.2.cloned.1.call-start
  19.5 0.0 copy-start
  19.5 1.6 copy-done
  21.1 1.0 deal.1
  22.1 0.0 copy-start.1
  22.1 2.9 %collective-permute-start = (bf16[256,2048]{1,0:T(8,128)(2,1)}, bf16[256,2048]{1,0:T(8,128)(2,1)S(1)}, u32[]{:S(2)}, u32[]{:S(2)}) collective-permute-start(bf16[256,2048]{1,0:T(8,128)(2,1)} %deal.1), channel_id=1, source_target_pairs={{0,8},{8,0},{1,9},{9,1},{2,10},{10,2},{3,11},{11,3},{4,12},{12,4},... | collective-permute-start | bytes 3145736 | tf_op jit(solution)/shard_map/ppermute | solution.py:323
  24.9 41.3 %conditional.2 = (bf16[64,32,128]{2,1,0:T(8,128)(2,1)}) conditional(s32[]{:T(128)} %convert_element_type.4, () %tuple.26, (bf16[16,128,128]{2,1,0:T(8,128)(2,1)}) %tuple.34), branch_computations={%region_0.0_spmd, %region_1.0_spmd} | conditional | flops 8388608 | bytes 2097160 | solution.py:335
  25.0 1.2 turn.1
  26.2 40.0 %all_to_all.37 = bf16[64,32,128]{2,1,0:T(8,128)(2,1)} all-to-all(bf16[64,32,128]{2,1,0:T(8,128)(2,1)S(1)} %turn.1), channel_id=1, replica_groups=mesh['x'=4,'yhi'=2,'core'=2,'ypair'=2,'yside'=2,'z'=8] {'x','yhi','core'..., dimensions={0} | all-to-all | bytes 1048576 | tf_op jit(solution)/shard_map/cond/branch_1_fun/all_to_all | solution.py:27
  66.2 0.0 collective-permute-done.got_ref
  66.2 0.3 all-gather.3.cloned.1.call-done
  66.5 0.0 copy-done.1
  66.5 0.0 copy-start.2
  66.5 1.6 copy-done.2
  68.1 0.0 copy-start.3
  68.1 0.8 project.1.turned_ref
  68.9 3.4 %collective-permute-start.1 = (bf16[256,256]{1,0:T(8,128)(2,1)S(1)}, bf16[256,256]{1,0:T(8,128)(2,1)S(1)}, u32[]{:S(2)}, u32[]{:S(2)}) collective-permute-start(bf16[256,256]{1,0:T(8,128)(2,1)S(1)} %project.1.turned_ref), channel_id=1, source_target_pairs={{0,8},{8,0},{1,9},{9,1},{2,10},{10,2},{3,11},{11,3},{4,12},{12,4},... | collective-permute-start | bytes 393224 | tf_op jit(solution)/shard_map/ppermute | solution.py:323
  72.3 0.0 copy-done.3
  72.3 0.4 moved.1.refs_1_
  72.7 1.9 collective-permute-done.1.other_ref
  74.6 0.7 tokens.1
  75.3 0.0 copy-start.5
  75.3 43.6 %all_to_all.41.refs_0_ = bf16[16,256,128]{2,1,0:T(8,128)(2,1)S(1)} all-to-all(bf16[16,256,128]{2,1,0:T(8,128)(2,1)S(1)} %tokens.1), channel_id=1, replica_groups=mesh['x'=4,'yhi'=2,'core'=2,'ypair'=2,'yside'=2,'z'=8] {'ypair','z'}, dimensions={0} | all-to-all | bytes 2097152 | tf_op jit(solution)/shard_map/all_to_all | solution.py:27
  118.9 0.9 applied.1
  119.8 16.4 %all_to_all.42.applied_ref = f32[4,128,256]{2,1,0:T(8,128)S(1)} all-to-all(f32[4,128,256]{2,1,0:T(8,128)S(1)} %get-tuple-element.33), channel_id=1, replica_groups=mesh['x'=4,'yhi'=2,'core'=2,'ypair'=2,'yside'=2,'z'=8] {'ypair','yside'}, dimensions={0} | all-to-all | bytes 1048576 | tf_op jit(solution)/shard_map/all_to_all | solution.py:27
  136.2 0.0 copy-done.5
  136.2 1.2 cross.1
  137.4 0.0 reduce-scatter.2.cloned.1.call-update
  137.5 0.6 gram.1
  138.1 37.6 %conditional.3 = ((f32[256,256]{1,0:T(8,128)S(1)}, bf16[1,256]{1,0:T(2,128)(2,1)}, f32[1,256]{1,0:T(1,128)S(1)})) conditional(s32[]{:T(128)} %convert_element_type.4, () %tuple.31, f32[256,256]{1,0:T(8,128)S(1)} %gram.1), branch_computations={%region_2.0_spmd, %region_3.0_spmd} | conditional | flops 10745806848 | bytes 3145736 | solution.py:393
  138.1 14.1 %all_to_all.38.parts_ref = f32[8,32,256]{2,1,0:T(8,128)S(1)} all-to-all(f32[8,32,256]{2,1,0:T(8,128)S(1)} %bitcast.17), channel_id=1, replica_groups=mesh['x'=4,'yhi'=2,'core'=2,'ypair'=2,'yside'=2,'z'=8] {'z'}, dimensions={0} | all-to-all | bytes 524288 | tf_op jit(solution)/shard_map/cond/branch_1_fun/all_to_all | solution.py:27
  152.2 13.2 %all_to_all.39 = f32[8,32,256]{2,1,0:T(8,128)S(1)} all-to-all(f32[8,32,256]{2,1,0:T(8,128)S(1)} %sum.1), channel_id=1, replica_groups=mesh['x'=4,'yhi'=2,'core'=2,'ypair'=2,'yside'=2,'z'=8] {'z'}, dimensions={0} | all-to-all | bytes 524288 | tf_op jit(solution)/shard_map/cond/branch_1_fun/all_to_all | solution.py:27
  165.4 10.2 %factor.1 = (f32[256,256]{1,0:T(8,128)S(1)}, bf16[1,256]{1,0:T(2,128)(2,1)}, f32[1,256]{1,0:T(1,128)S(1)}) custom-call(f32[256,256]{1,0:T(8,128)S(1)} %bitcast.16), custom_call_target="tpu_custom_call" | custom-call | flops 10737418240 | bytes 1048576 | tf_op jit(solution)/shard_map/cond/branch_1_fun/factor/pallas_call | solution.py:391
  175.7 1.3 fresh.1
  176.9 0.0 reduce-scatter.2.cloned.1.call-done.cross_ref
  176.9 0.0 copy-start.4
  176.9 0.8 copy-done.4
  177.8 0.4 scale.1
  178.2 11.8 %all_to_all.43.scaled_ref = bf16[8,64,256]{2,1,0:T(8,128)(2,1)S(1)} all-to-all(bf16[8,64,256]{2,1,0:T(8,128)(2,1)S(1)} %scale.1), channel_id=1, replica_groups=mesh['x'=4,'yhi'=2,'core'=2,'ypair'=2,'yside'=2,'z'=8] {'z'}, dimensions={0} | all-to-all | bytes 524288 | tf_op jit(solution)/shard_map/all_to_all | solution.py:27
  190.0 0.4 result.1
  190.4 28.2 %all_to_all.44.turned_ref = bf16[64,32,128]{2,1,0:T(8,128)(2,1)S(1)} all-to-all(bf16[64,32,128]{2,1,0:T(8,128)(2,1)S(1)} %result.1), channel_id=1, replica_groups=mesh['x'=4,'yhi'=2,'core'=2,'ypair'=2,'yside'=2,'z'=8] {'x','yhi','core'..., dimensions={0} | all-to-all | bytes 1048576 | tf_op jit(solution)/shard_map/all_to_all | solution.py:27
  218.6 1.0 turn_back.1
  (1 shorter events, 0.0 us)
Async XLA Ops:
  7.2 59.4 %all-gather.3.cloned.1.call-start = ((), (), s32[]{:S(2)}) async-start(), calls=%async_computation.10 | async-start | bytes 2359296 | tf_op jit(solution)/shard_map/all_gather | solution.py:317
  19.4 157.5 %reduce-scatter.2.cloned.1.call-start = ((), (), s32[]{:S(2)}) async-start(), calls=%async_computation.9 | async-start | bytes 589824 | tf_op jit(solution)/shard_map/reduce_scatter | solution.py:377
  19.5 1.6 copy-start
  22.1 44.5 %copy-start.1 = (bf16[1,256,4096]{2,1,0:T(8,128)(2,1)S(1)}, bf16[1,256,4096]{2,1,0:T(8,128)(2,1)}, u32[]{:S(2)}) copy-start(bf16[1,256,4096]{2,1,0:T(8,128)(2,1)} %param.8) | copy-start | bytes 6291460
  22.1 44.1 %collective-permute-start = (bf16[256,2048]{1,0:T(8,128)(2,1)}, bf16[256,2048]{1,0:T(8,128)(2,1)S(1)}, u32[]{:S(2)}, u32[]{:S(2)}) collective-permute-start(bf16[256,2048]{1,0:T(8,128)(2,1)} %deal.1), channel_id=1, source_target_pairs={{0,8},{8,0},{1,9},{9,1},{2,10},{10,2},{3,11},{11,3},{4,12},{12,4},... | collective-permute-start | bytes 3145736 | tf_op jit(solution)/shard_map/ppermute | solution.py:323
  66.5 1.6 copy-start.2
  68.1 4.1 %copy-start.3 = (bf16[1,128,4096]{2,1,0:T(8,128)(2,1)S(1)}, bf16[1,128,4096]{2,1,0:T(8,128)(2,1)}, u32[]{:S(2)}) copy-start(bf16[1,128,4096]{2,1,0:T(8,128)(2,1)} %param.9) | copy-start | bytes 3145732
  68.9 5.7 %collective-permute-start.1 = (bf16[256,256]{1,0:T(8,128)(2,1)S(1)}, bf16[256,256]{1,0:T(8,128)(2,1)S(1)}, u32[]{:S(2)}, u32[]{:S(2)}) collective-permute-start(bf16[256,256]{1,0:T(8,128)(2,1)S(1)} %project.1.turned_ref), channel_id=1, source_target_pairs={{0,8},{8,0},{1,9},{9,1},{2,10},{10,2},{3,11},{11,3},{4,12},{12,4},... | collective-permute-start | bytes 393224 | tf_op jit(solution)/shard_map/ppermute | solution.py:323
  75.3 60.9 %copy-start.5 = (bf16[64,32,128]{2,1,0:T(8,128)(2,1)S(1)}, bf16[64,32,128]{2,1,0:T(8,128)(2,1)}, u32[]{:S(2)}) copy-start(bf16[64,32,128]{2,1,0:T(8,128)(2,1)} %get-tuple-element.53.slab_ref) | copy-start | bytes 1572868
  176.9 0.8 copy-start.4
Sparse Core Ops, SparseCore 0:
  19.5 46.9 all-gather.2
  137.6 32.7 reduce-scatter.1
